TPU v7x, 128 devices: a whole 4x4x4 slice. The times are simulated.
128 devices in a mesh: row: 16 (over z, x), col: 8 (over y, core).
Axes of the slice: x: 4, y: 4, z: 4, core: 2. Of those that a mesh axis runs over, the one named last changes fastest.
Arguments:
- blocks: float32 [8192, 4, 128, 128], P(('row', 'col')), may hold values from -0.25 to 0.25
- block_cols: int32 [8192, 4], P(('row', 'col')), may hold values from 0 to 1023, as said below
- targets: float32 [32, 1048576], P(None, ('row', 'col')), may hold values from -6 to 6
Outputs:
- solution: float32 [32, 131072], P(None, ('row', 'col'))
- residual: float32 [32, 1048576], P(None, ('row', 'col'))
Inputs may be any that keep to these rules, and one draw needn't show every extreme that they name: `block_cols`: the four indices of a block row differ. Block row i belongs to device d = i // 64, devices numbered row-major over (row, col); every index j of it satisfies (j // 8) % 8 == d % 8.
All inputs are finite; a program needn't handle non-finite values.
Results may differ from a plain program's by a relative error of at most 0.00012.
Values sent between devices are 32-bit elements; how exact they have to be, the bound alone decides.
A program may use at most 128 MiB of HBM per device.

v0:
```python
import jax
import jax.numpy as jnp
from jax import lax
from jax.sharding import PartitionSpec as P

ITERS = 3
CBD = 8


def chol_solve(matrix, right):
    lower_factor = jnp.linalg.cholesky(matrix)
    middle = lax.linalg.triangular_solve(lower_factor, right, left_side=True, lower=True)
    return lax.linalg.triangular_solve(
        lower_factor, middle, left_side=True, lower=True, transpose_a=True
    )


def gram_of(matrix):
    return jnp.dot(
        matrix, matrix.T, precision=lax.Precision.HIGHEST, preferred_element_type=jnp.float32
    )


def body(blocks, block_cols, targets):
    row_count = lax.axis_size("row")
    col_count = lax.axis_size("col")
    block_rows = blocks.shape[0]
    tile_size = blocks.shape[2]
    rhs_count = targets.shape[0]
    group_size = CBD * row_count
    flat_cols = block_cols.reshape(-1)
    local_cols = flat_cols // CBD // col_count * CBD + flat_cols % CBD

    def backward(resid):
        shaped = resid.reshape(rhs_count, block_rows, tile_size)
        pieces_all = jnp.einsum("ikab,nia->iknb", blocks, shaped, precision=lax.Precision.HIGHEST)
        pieces_all = pieces_all.reshape(block_rows * 4, rhs_count, tile_size)
        summed = jax.ops.segment_sum(pieces_all, local_cols, num_segments=group_size)
        return summed.transpose(1, 0, 2).reshape(rhs_count, group_size * tile_size)

    def gradient_of(resid):
        gradient = lax.psum(backward(resid), "row")
        total_gram = lax.psum(gram_of(gradient), "col")
        return (gradient, total_gram)

    residual = targets
    gradient, grad_gram = gradient_of(residual)
    direction = gradient
    solution = jnp.zeros(direction.shape, jnp.float32)
    for iteration in range(ITERS):
        gathered = direction
        tiles = gathered.reshape(rhs_count, group_size, tile_size)
        picked = jnp.take(tiles, local_cols, axis=1).reshape(rhs_count, block_rows, 4, tile_size)
        image = jnp.einsum("ikab,nikb->nia", blocks, picked, precision=lax.Precision.HIGHEST)
        image = image.reshape(rhs_count, block_rows * tile_size)
        image_gram = lax.psum(gram_of(image), ("row", "col"))
        step_size = chol_solve(image_gram, grad_gram)
        solution = solution + jnp.dot(step_size.T, direction, precision=lax.Precision.HIGHEST)
        residual = residual - jnp.dot(step_size.T, image, precision=lax.Precision.HIGHEST)
        if iteration + 1 < ITERS:
            gradient, new_gram = gradient_of(residual)
            mix = chol_solve(grad_gram, new_gram)
            direction = gradient + jnp.dot(mix.T, direction, precision=lax.Precision.HIGHEST)
            grad_gram = new_gram
    width = CBD * tile_size
    solution = lax.dynamic_slice_in_dim(solution, lax.axis_index("row") * width, width, 1)
    return (solution, residual)


def solution(mesh):
    placed = (P(("row", "col"), None, None, None), P(("row", "col"), None), P(None, ("row", "col")))
    return jax.shard_map(
        body,
        mesh=mesh,
        in_specs=placed,
        out_specs=(P(None, ("row", "col")), P(None, ("row", "col"))),
        check_vma=False,
    )
```

profile of v0, /device:TPU:1, one launch (start us, length us, event | category | flops | bytes accessed | tf_op | source)
XLA Modules:
  0.0 828.7 jit_solution(4298627936021368417)
XLA Ops:
  9.5 13.1 %fusion.13 = f32[64,32,4,128]{3,1,2,0:T(8,128)} fusion(f32[64,4,128,128]{3,2,1,0:T(8,128)} %param.10, f32[32,64,128,1]{2,1,0,3:T(8,128)S(1)} %bitcast.221), kind=kOutput, calls=%fused_computation.36 | convolution fusion | flops 1610612736 | bytes 22020096 | tf_op jit(solution)/shard_map/ikab,nia->iknb/dot_general | solution.py:36
  22.8 22.4 %scatter_fusion = f32[128,32,128]{2,1,0:T(8,128)S(1)} fusion(f32[128,32,128]{2,1,0:T(8,128)S(1)} %broadcast.181.clone, s32[256]{0:T(256)S(1)} %bitcast.224, f32[256,32,128]{2,1,0:T(8,128)} %bitcast.213), kind=kCustom, calls=%fused_computation.3 | custom fusion | flops 1048576 | bytes 12583936 | tf_op jit(solution)/shard_map/scatter-add | solution.py:38
  47.0 92.5 %all-reduce.4.cloned.1.call-done = f32[32,16384]{1,0:T(8,128)} async-done(((f32[32,16384]{1,0:T(8,128)}), f32[32,16384]{1,0:T(8,128)}) %all-reduce.4.cloned.1.call-update) | async-done | bytes 2097168 | tf_op jit(solution)/shard_map/psum | solution.py:42
  141.3 3.0 gather_fusion
  147.0 19.5 %fusion.47 = f32[64,32,128,1]{2,1,3,0:T(8,128)S(1)} fusion(f32[32,64,4,128]{3,0,2,1:T(8,128)S(1)} %bitcast.216, f32[64,4,128,128]{3,2,1,0:T(8,128)} %param.10), kind=kOutput, calls=%fused_computation.115 | convolution fusion | flops 1610612736 | bytes 22020096 | tf_op jit(solution)/shard_map/ikab,nikb->nia/dot_general | solution.py:54
  167.5 66.0 %psum.64 = f32[32,32]{0,1:T(8,128)S(1)} all-reduce(f32[32,32]{0,1:T(8,128)S(1)} %convolution_bitcast_fusion.2), channel_id=1, replica_groups=mesh['row'=16,'col'=8] {'row','col'}, use_global_device_ids=true, to_apply=%region_2.4 | all-reduce | flops 1024 | bytes 8192 | tf_op jit(solution)/shard_map/psum | solution.py:56
  233.5 2.9 cholesky.89
  242.0 20.9 %psum.65 = f32[32,32]{0,1:T(8,128)S(1)} all-reduce(f32[32,32]{0,1:T(8,128)S(1)} %fusion.48), channel_id=1, replica_groups=mesh['row'=16,'col'=8] {'col'}, use_global_device_ids=true, to_apply=%region_5.8 | all-reduce | flops 1024 | bytes 8192 | tf_op jit(solution)/shard_map/psum | solution.py:43
  266.8 13.0 %fusion.10 = f32[64,32,4,128]{3,1,2,0:T(8,128)} fusion(f32[64,4,128,128]{3,2,1,0:T(8,128)} %param.10, f32[32,64,128,1]{2,1,0,3:T(8,128)S(1)} %bitcast.222), kind=kOutput, calls=%fused_computation.33 | convolution fusion | flops 1610612736 | bytes 22020096 | tf_op jit(solution)/shard_map/ikab,nia->iknb/dot_general | solution.py:36
  281.4 34.0 %scatter_fusion.1 = f32[128,32,128]{2,1,0:T(8,128)} fusion(f32[128,32,128]{2,1,0:T(8,128)} %broadcast.181.clone.1, s32[256]{0:T(256)S(1)} %bitcast.225, f32[256,32,128]{2,1,0:T(8,128)} %bitcast.214), kind=kCustom, calls=%fused_computation.4 | custom fusion | flops 1048576 | bytes 12583936 | tf_op jit(solution)/shard_map/scatter-add | solution.py:38
  315.4 3.1 copy_bitcast_fusion.1
  318.6 2.9 cholesky.100
  325.3 81.3 %all-reduce.6.cloned.1.call-done = f32[32,16384]{1,0:T(8,128)} async-done(((f32[32,16384]{1,0:T(8,128)}), f32[32,16384]{1,0:T(8,128)}) %all-reduce.6.cloned.1.call-update) | async-done | bytes 2097168 | tf_op jit(solution)/shard_map/psum | solution.py:42
  406.6 4.0 fusion.50
  410.7 23.0 %psum.67 = f32[32,32]{0,1:T(8,128)S(1)} all-reduce(f32[32,32]{0,1:T(8,128)S(1)} %fusion.50), channel_id=1, replica_groups=mesh['row'=16,'col'=8] {'col'}, use_global_device_ids=true, to_apply=%region_8.13 | all-reduce | flops 1024 | bytes 8192 | tf_op jit(solution)/shard_map/psum | solution.py:43
  434.0 3.6 convolution_add_fusion.1
  440.5 4.3 gather_fusion.1
  447.6 19.3 %fusion.51 = f32[64,32,128,1]{2,1,3,0:T(8,128)S(1)} fusion(f32[32,64,4,128]{3,0,2,1:T(8,128)S(1)} %bitcast.217, f32[64,4,128,128]{3,2,1,0:T(8,128)} %param.10), kind=kOutput, calls=%fused_computation.119 | convolution fusion | flops 1610612736 | bytes 22020096 | tf_op jit(solution)/shard_map/ikab,nikb->nia/dot_general | solution.py:54
  468.9 65.3 %psum.68 = f32[32,32]{0,1:T(8,128)S(1)} all-reduce(f32[32,32]{0,1:T(8,128)S(1)} %convolution_bitcast_fusion.1), channel_id=1, replica_groups=mesh['row'=16,'col'=8] {'row','col'}, use_global_device_ids=true, to_apply=%region_9.14 | all-reduce | flops 1024 | bytes 8192 | tf_op jit(solution)/shard_map/psum | solution.py:56
  544.2 13.1 %fusion.7 = f32[64,32,4,128]{3,1,2,0:T(8,128)} fusion(f32[64,4,128,128]{3,2,1,0:T(8,128)} %param.10, f32[32,64,128,1]{2,1,0,3:T(8,128)S(1)} %bitcast.223), kind=kOutput, calls=%fused_computation.30 | convolution fusion | flops 1610612736 | bytes 22020096 | tf_op jit(solution)/shard_map/ikab,nia->iknb/dot_general | solution.py:36
  558.8 34.2 %scatter_fusion.2 = f32[128,32,128]{2,1,0:T(8,128)} fusion(f32[128,32,128]{2,1,0:T(8,128)} %broadcast.181, s32[256]{0:T(256)S(1)} %bitcast.226, f32[256,32,128]{2,1,0:T(8,128)} %bitcast.212), kind=kCustom, calls=%fused_computation.5 | custom fusion | flops 1048576 | bytes 12583936 | tf_op jit(solution)/shard_map/scatter-add | solution.py:38
  593.0 3.0 copy_bitcast_fusion
  596.1 3.3 fusion.49
  606.1 4.9 fusion.52
  611.0 71.5 %all-reduce.8.cloned.1.call-done = f32[32,16384]{1,0:T(8,128)} async-done(((f32[32,16384]{1,0:T(8,128)}), f32[32,16384]{1,0:T(8,128)}) %all-reduce.8.cloned.1.call-update) | async-done | bytes 2097168 | tf_op jit(solution)/shard_map/psum | solution.py:42
  682.5 4.0 fusion.53
  686.6 23.1 %psum.70 = f32[32,32]{1,0:T(8,128)S(1)} all-reduce(f32[32,32]{1,0:T(8,128)S(1)} %fusion.53), channel_id=1, replica_groups=mesh['row'=16,'col'=8] {'col'}, use_global_device_ids=true, to_apply=%region_12.17 | all-reduce | flops 1024 | bytes 8192 | tf_op jit(solution)/shard_map/psum | solution.py:43
  710.0 3.6 convolution_add_fusion
  715.2 3.0 gather_fusion.2
  720.9 19.3 %fusion.54 = f32[64,32,128,1]{2,1,3,0:T(8,128)S(1)} fusion(f32[32,64,4,128]{3,0,2,1:T(8,128)S(1)} %bitcast.215, f32[64,4,128,128]{3,2,1,0:T(8,128)} %param.10), kind=kOutput, calls=%fused_computation.122 | convolution fusion | flops 1610612736 | bytes 22020096 | tf_op jit(solution)/shard_map/ikab,nikb->nia/dot_general | solution.py:54
  742.2 65.4 %psum.71 = f32[32,32]{0,1:T(8,128)S(1)} all-reduce(f32[32,32]{0,1:T(8,128)S(1)} %convolution_bitcast_fusion), channel_id=1, replica_groups=mesh['row'=16,'col'=8] {'row','col'}, use_global_device_ids=true, to_apply=%region_13.18 | all-reduce | flops 1024 | bytes 8192 | tf_op jit(solution)/shard_map/psum | solution.py:56
  814.8 3.2 convolution_subtract_fusion
  (92 shorter events, 68.2 us)
Async XLA Ops:
  7.2 132.3 %all-reduce.4.cloned.1.call-start = ((), (), s32[]{:S(2)}) async-start(), calls=%async_computation | async-start | bytes 4194304 | tf_op jit(solution)/shard_map/psum | solution.py:42
  46.8 359.8 %all-reduce.6.cloned.1.call-start = ((), (), s32[]{:S(2)}) async-start(), calls=%async_computation.1 | async-start | bytes 4194304 | tf_op jit(solution)/shard_map/psum | solution.py:42
  147.0 93.2 %copy-start = (f32[32,16384]{1,0:T(8,128)S(1)}, f32[32,16384]{1,0:T(8,128)}, u32[]{:S(2)}) copy-start(f32[32,16384]{1,0:T(8,128)} %all-reduce.4.cloned.1.call-done) | copy-start | bytes 6291460
  265.6 1.0 copy-start.5
  318.5 364.0 %all-reduce.8.cloned.1.call-start = ((), (), s32[]{:S(2)}) async-start(), calls=%async_computation.2 | async-start | bytes 4194304 | tf_op jit(solution)/shard_map/psum | solution.py:42
  437.6 1.3 copy-start.1
  466.9 1.0 copy-start.7
  611.0 99.0 %copy-start.2 = (f32[32,16384]{1,0:T(8,128)S(1)}, f32[32,16384]{1,0:T(8,128)}, u32[]{:S(2)}) copy-start(f32[32,16384]{1,0:T(8,128)} %copy-done.1) | copy-start | bytes 6291460
  713.6 1.3 copy-start.3
  740.2 1.0 copy-start.6
  741.2 76.8 %copy-start.4 = (f32[32,16384]{1,0:T(8,128)S(1)}, f32[32,16384]{1,0:T(8,128)}, u32[]{:S(2)}) copy-start(f32[32,16384]{1,0:T(8,128)} %copy-done.3) | copy-start | bytes 6291460
Sparse Core Ops, SparseCore 0:
  46.9 92.5 all-reduce.3
  318.6 87.9 all-reduce.5
  596.2 86.2 all-reduce.7
where the time goes:
time: 837 us; the launch traced here: 829 us
  blocking collectives  264 us (32%)
  waiting for transfers between devices  245 us (29%)
  matrix products  137 us (16%)
  other arithmetic  134 us (16%)
  local copies, waits for them, and re-layouts  33.8 us (4%)
  between operations  14.7 us (2%)
    psum x3, waiting for transfers between devices, gradient_of(): gradient = lax.psum(backward(resid), 'row')  245 us
    psum x3, blocking collectives, body(): image_gram = lax.psum(gram_of(image), ('row', 'col'))  197 us
    scatter-add x3, other arithmetic, backward(): jax.ops.segment_sum(pieces_all, local_cols, num_segments=group_size)  90.6 us
    psum x3, blocking collectives, gradient_of(): total_gram = lax.psum(gram_of(gradient), 'col')  67.1 us
    dot_general x3, matrix products, body(): jnp.einsum('ikab,nikb->nia', blocks, picked, precision=lax.Precision.HIGH...  58.2 us
    dot_general x3, matrix products, backward(): jnp.einsum('ikab,nia->iknb', blocks, shaped, precision=lax.Precision.HIGH...  39.2 us
    another operation x15, other arithmetic, chol_solve(): lower_factor = jnp.linalg.cholesky(matrix)  18 us
  transfers between devices with their start and end apart: 3, of which 3 were waited for; matrix products, arithmetic and copies ran while one was open for 3% of the time, Pallas kernels for 0%

commit v1 on v0

v1 whole, which is shorter than its diff:
```python
import functools

import jax
import jax.numpy as jnp
from jax import lax
from jax.experimental import pallas as pl
from jax.experimental.pallas import tpu as pltpu
from jax.sharding import PartitionSpec as P

MESH = pl.DeviceIdType.MESH
F32 = jnp.float32
BF16 = jnp.bfloat16
ITERS = 3
CBD = 8
N = 32
B = 128
STEP_ROWS = 8
MIB = 2**20


def dot(a, b, ca, cb, precision=None):
    return lax.dot_general(
        a, b, (((ca,), (cb,)), ((), ())), precision=precision, preferred_element_type=F32
    )


def exact(a, b, ca=1, cb=0):
    return dot(a, b, ca, cb, lax.Precision.HIGHEST)


def split(x):
    hi = x.astype(BF16)
    lo = (x - hi.astype(F32)).astype(BF16)
    return hi, lo


def stacked(x):
    hi, lo = split(x)
    return jnp.concatenate([hi, lo], axis=0)


def local_kernel(forward, backward, earlier, cols, *refs):
    refs = list(refs)
    blocks = refs.pop(0)
    vec = refs.pop(0)
    before = [refs.pop(0) for _ in range(earlier)]
    image_out = refs.pop(0) if forward else None
    gram_out = refs.pop(0) if forward else None
    sums = refs.pop(0) if backward else None
    parts = refs.pop(0) if forward else None
    gram_acc = refs.pop(0) if forward else None
    step = pl.program_id(0)

    @pl.when(step == 0)
    def _():
        if backward:
            sums[...] = jnp.zeros_like(sums)
        if forward:
            gram_acc[...] = jnp.zeros_like(gram_acc)

            def cut(c, carry):
                hi, lo = split(vec[c])
                parts[c, 0:N, :] = hi
                parts[c, N : 2 * N, :] = lo
                return carry

            lax.fori_loop(0, vec.shape[0], cut, 0, unroll=4)

    for i in range(STEP_ROWS):
        base = (step * STEP_ROWS + i) * 4
        at = slice(i * B, (i + 1) * B)
        tiles = [stacked(blocks[i, k]) for k in range(4)]
        if forward:
            picked = jnp.concatenate([parts[cols[base + k]] for k in range(4)], axis=1)
            quad = dot(picked, jnp.concatenate(tiles, axis=1), 1, 1)
            quad = quad[:N] + quad[N:]
            image = quad[:, :B] + quad[:, B:]
            image_out[:, at] = image
        else:
            image = vec[:, at]
        both = stacked(image)
        if forward:
            others = [both] + [stacked(e[:, at]) for e in before]
            gram_acc[:, : 2 * N * len(others)] += dot(
                both, jnp.concatenate(others, axis=0), 1, 1
            )
        if backward:
            wide = jnp.concatenate([both, both], axis=1)
            piece = dot(wide, jnp.concatenate(tiles, axis=1), 1, 0)
            piece = piece[:N] + piece[N:]
            for k in range(4):
                c = cols[base + k]
                sums[c] += piece[:, k * B : (k + 1) * B]

    if forward:

        @pl.when(step == pl.num_programs(0) - 1)
        def _():
            gram_out[...] = jnp.zeros_like(gram_out)
            for j in range(earlier + 1):
                q = gram_acc[:, 2 * N * j : 2 * N * (j + 1)]
                q = q[:N] + q[N:]
                gram_out[:, N * (j + 1) : N * (j + 2)] = q[:, :N] + q[:, N:]


def local_pass(forward, backward, cols, blocks, vec, before, group):
    rows = blocks.shape[0]
    width = STEP_ROWS * B
    strip = pl.BlockSpec((N, width), lambda s, c: (0, s))
    whole = pl.BlockSpec((group, N, B), lambda s, c: (0, 0, 0))
    outs, out_specs, scratch = [], [], []
    if forward:
        outs += [jax.ShapeDtypeStruct((N, rows * B), F32), jax.ShapeDtypeStruct((N, B), F32)]
        out_specs += [strip, pl.BlockSpec((N, B), lambda s, c: (0, 0))]
        scratch += [pltpu.VMEM((group, 2 * N, B), BF16), pltpu.VMEM((2 * N, 2 * B), F32)]
    if backward:
        outs += [jax.ShapeDtypeStruct((group, N, B), F32)]
        out_specs += [whole]
    return pl.pallas_call(
        functools.partial(local_kernel, forward, backward, len(before)),
        grid_spec=pltpu.PrefetchScalarGridSpec(
            num_scalar_prefetch=1,
            grid=(rows // STEP_ROWS,),
            in_specs=[
                pl.BlockSpec((STEP_ROWS, 4, B, B), lambda s, c: (s, 0, 0, 0)),
                whole if forward else strip,
            ]
            + [strip] * len(before),
            out_specs=out_specs,
            scratch_shapes=scratch,
        ),
        out_shape=outs,
        compiler_params=pltpu.CompilerParams(vmem_limit_bytes=48 * MIB),
    )(cols, blocks, vec, *before)


def spd_solve(matrix, right):
    table = jnp.concatenate([matrix, right], axis=1)
    row_id = lax.broadcasted_iota(jnp.int32, table.shape, 0)
    for k in range(N):
        row = table[k : k + 1, :] / table[k : k + 1, k : k + 1]
        table = jnp.where(row_id == k, row, table - table[:, k : k + 1] * row)
    return table[:, N : 2 * N]


class Traffic:
    def __init__(self, send_sem, recv_sem):
        self.send_sem, self.recv_sem = send_sem, recv_sem
        self.sent = []

    def send(self, slot, src, dst, device):
        copy = pltpu.make_async_remote_copy(
            src_ref=src,
            dst_ref=dst,
            send_sem=self.send_sem.at[slot],
            recv_sem=self.recv_sem.at[slot],
            device_id=device,
            device_id_type=MESH,
        )
        copy.start()
        self.sent.append(copy)
        return copy

    def finish(self):
        for copy in self.sent:
            copy.wait_send()


OFFSETS = (2, 3, 1, 0)


def places(n_x):
    row = lax.axis_index("row")
    col = lax.axis_index("col")
    z, x = row // n_x, lax.rem(row, n_x)

    def along_x(d):
        return (z * n_x + lax.rem(x + d, n_x), col)

    def along_z(d):
        return (lax.rem(z + d, 4) * n_x + x, col)

    return row, col, z, x, along_x, along_z


def reduce_scatter_start(work, z, x, along_x, along_z, r1, tr):
    cps = {}
    for u in range(4):
        for h in range(2):
            pa, pb, ring = (x, z, along_x) if h == 0 else (z, x, along_z)
            tb = lax.rem(pb + OFFSETS[u], 4)

            def src(ta, s, h=h, tb=tb):
                ta = lax.rem(ta, 4)
                return work(h, ta, tb, s)

            base = (h * 4 + u) * 6
            for idx, ta, s, d in ((0, pa + 2, 0, 1), (1, pa + 2, 1, 3), (2, pa + 1, 1, 1), (3, pa + 3, 0, 3)):
                cps[h, u, idx] = tr.send(base + idx, src(ta, s), r1.at[h, u, idx], ring(d))
    return cps


def reduce_scatter_rest(work, z, x, along_x, along_z, r1, p1, r2, tr, cps, hook):
    c2 = {}
    halves = ((x, z, along_x, along_z), (z, x, along_z, along_x))

    def pass_on(u, h):
        pa, pb, ring, _ = halves[h]
        tb = lax.rem(pb + OFFSETS[u], 4)
        base = (h * 4 + u) * 6
        cps[h, u, 0].wait_recv()
        r1[h, u, 0] += work(h, lax.rem(pa + 1, 4), tb, 0)[...]
        cps[h, u, 4] = tr.send(base + 4, r1.at[h, u, 0], r1.at[h, u, 4], ring(1))
        cps[h, u, 1].wait_recv()
        r1[h, u, 1] += work(h, lax.rem(pa + 3, 4), tb, 1)[...]
        cps[h, u, 5] = tr.send(base + 5, r1.at[h, u, 1], r1.at[h, u, 5], ring(3))

    def close(u, h):
        pa, pb, _, ring = halves[h]
        tb = lax.rem(pb + OFFSETS[u], 4)
        base = 48 + h * 6
        for idx in (2, 3, 4, 5):
            cps[h, u, idx].wait_recv()
        p1[h, u, 0:2] = work(h, pa, tb, 0)[...] + (r1[h, u, 3] + r1[h, u, 4])
        p1[h, u, 2:4] = work(h, pa, tb, 1)[...] + (r1[h, u, 2] + r1[h, u, 5])
        if u == 0:
            c2[h, 0] = tr.send(base + 0, p1.at[h, 0, pl.ds(0, 2)], r2.at[h, 0], ring(1))
            c2[h, 1] = tr.send(base + 1, p1.at[h, 0, pl.ds(2, 2)], r2.at[h, 1], ring(3))
        if u == 1:
            c2[h, 3] = tr.send(base + 3, p1.at[h, 1, pl.ds(0, 2)], r2.at[h, 3], ring(3))
            c2[h, 1].wait_recv()
            r2[h, 1] += p1[h, 1, 2:4]
            c2[h, 5] = tr.send(base + 5, r2.at[h, 1], r2.at[h, 5], ring(3))
        if u == 2:
            c2[h, 2] = tr.send(base + 2, p1.at[h, 2, pl.ds(2, 2)], r2.at[h, 2], ring(1))
            c2[h, 0].wait_recv()
            r2[h, 0] += p1[h, 2, 0:2]
            c2[h, 4] = tr.send(base + 4, r2.at[h, 0], r2.at[h, 4], ring(1))

    for u in range(5):
        if u < 4:
            for h in range(2):
                pass_on(u, h)
        if u >= 1:
            for h in range(2):
                close(u - 1, h)
        hook(u)
    own = []
    for h in range(2):
        for idx in (2, 3, 4, 5):
            c2[h, idx].wait_recv()
        first = p1[h, 3, 0:2] + (r2[h, 3] + r2[h, 4])
        second = p1[h, 3, 2:4] + (r2[h, 2] + r2[h, 5])
        own += [first[0], first[1], second[0], second[1]]
    return jnp.concatenate(own, axis=1)


def gather_all(place, z, x, along_x, along_z, tr, base0):
    halves = ((x, z, along_x, along_z), (z, x, along_z, along_x))
    c1, c2 = {}, {}
    order = (0, 3, 1, 2)

    def send1(h, idx):
        pa, pb, _, ring = halves[h]
        off, s, d = ((0, None, 1), (0, None, 3), (3, 0, 1), (1, 1, 3))[idx]
        ref = place(h, pa, lax.rem(pb + off, 4), s)
        c1[h, idx] = tr.send(base0 + h * 4 + idx, ref, ref, ring(d))

    def send2(h, v, idx):
        pa, pb, ring, _ = halves[h]
        tb = lax.rem(pb + order[v], 4)
        off, s, d = ((0, None, 1), (0, None, 3), (3, 0, 1), (1, 1, 3))[idx]
        ref = place(h, lax.rem(pa + off, 4), tb, s)
        c2[h, v, idx] = tr.send(base0 + 8 + (h * 4 + v) * 4 + idx, ref, ref, ring(d))

    both = range(2)
    for h in both:
        send1(h, 0)
        send1(h, 1)
    for h in both:
        send2(h, 0, 0)
        send2(h, 0, 1)
    for h in both:
        c1[h, 0].wait_recv()
        send1(h, 2)
        send2(h, 1, 0)
        send2(h, 1, 1)
        c1[h, 1].wait_recv()
        send1(h, 3)
        send2(h, 2, 0)
        send2(h, 2, 1)
    for v in range(4):
        for h in both:
            if v == 1:
                c1[h, 2].wait_recv()
                c1[h, 3].wait_recv()
                send2(h, 3, 0)
                send2(h, 3, 1)
            c2[h, v, 0].wait_recv()
            send2(h, v, 2)
            c2[h, v, 1].wait_recv()
            send2(h, v, 3)
    for v in range(4):
        for h in both:
            c2[h, v, 2].wait_recv()
            c2[h, v, 3].wait_recv()


RS_SLOTS = 60
AG_SLOTS = 40


class GramSum:
    def __init__(self, row, col, n_row, n_col, tr, slot0, box1, box2):
        self.row, self.col, self.n_row, self.n_col = row, col, n_row, n_col
        self.tr, self.slot0, self.box1, self.box2 = tr, slot0, box1, box2

    def first(self, tile):
        self.box1[self.col] = tile
        self.c1 = []
        for d in range(1, self.n_col):
            ref = self.box1.at[self.col]
            to = (self.row, lax.rem(self.col + d, self.n_col))
            self.c1.append(self.tr.send(self.slot0 + d - 1, ref, ref, to))

    def second(self):
        for c in self.c1:
            c.wait_recv()
        total = self.box1[0]
        for i in range(1, self.n_col):
            total = total + self.box1[i]
        self.box2[self.row] = total
        self.c2 = []
        for d in range(1, self.n_row):
            ref = self.box2.at[self.row]
            to = (lax.rem(self.row + d, self.n_row), self.col)
            self.c2.append(self.tr.send(self.slot0 + self.n_col - 1 + d - 1, ref, ref, to))

    def total(self):
        for c in self.c2:
            c.wait_recv()
        total = self.box2[0]
        for i in range(1, self.n_row):
            total = total + self.box2[i]
        return total


def meet(row, col, n_row, n_col, along_x, along_z, grams):
    barrier = pltpu.get_barrier_semaphore()
    if grams:
        who = [(row, lax.rem(col + d, n_col)) for d in range(1, n_col)]
        who += [(lax.rem(row + d, n_row), col) for d in range(1, n_row)]
    else:
        who = [along_x(1), along_x(3), along_z(1), along_z(3)]
    for device in who:
        pl.semaphore_signal(barrier, inc=1, device_id=device, device_id_type=MESH)
    pl.semaphore_wait(barrier, len(who))


GG, IG, MIX1, STEP0, STEP1 = range(5)


def small_solves(k, total, state):
    gg = total[:, 0:N]
    image_gram = total[:, N : 2 * N]
    mix = None
    if k >= 2:
        mix = spd_solve(state[GG], gg)
        cross = total[:, 2 * N : 3 * N]
        if k == 3:
            cross = cross + exact(total[:, 3 * N : 4 * N], state[MIX1])
        mixed = exact(cross, mix)
        image_gram = image_gram + (mixed + mixed.T) + exact(mix, exact(state[IG], mix), 0, 0)
    step = spd_solve(image_gram, gg)
    return gg, image_gram, mix, step


def exchange_kernel(k, n_row, n_col, *refs):
    refs = list(refs)
    sums = refs.pop(0)
    if k:
        gram_in, tile_in, grad_in, state_in = (refs.pop(0) for _ in range(4))
    if k >= 2:
        conj_in = refs.pop(0)
    vec, grad_out, tile_out = (refs.pop(0) for _ in range(3))
    if k:
        conj_out, state_out = refs.pop(0), refs.pop(0)
    r1, p1, r2, send_sem, recv_sem = (refs.pop(0) for _ in range(5))
    if k:
        box1, box2 = refs.pop(0), refs.pop(0)
    row, col, z, x, along_x, along_z = places(n_row // 4)
    tr = Traffic(send_sem, recv_sem)
    meet(row, col, n_row, n_col, along_x, along_z, k > 0)

    def work(h, ta, tb, s):
        zz, xx = (tb, ta) if h == 0 else (ta, tb)
        return sums.at[zz, xx, h, pl.ds(2 * s, 2)]

    def place(h, ta, tb, s):
        zz, xx = (tb, ta) if h == 0 else (ta, tb)
        return vec.at[zz, xx, h] if s is None else vec.at[zz, xx, h, pl.ds(2 * s, 2)]

    if k:
        grams = GramSum(row, col, n_row, n_col, tr, RS_SLOTS + AG_SLOTS, box1, box2)
        grams.first(gram_in[...] + tile_in[...])
    cps = reduce_scatter_start(work, z, x, along_x, along_z, r1, tr)
    found = []

    def hook(u):
        if k and u == 0:
            grams.second()
        if k and u == 2:
            found.extend(small_solves(k, grams.total(), state_in))

    fresh = reduce_scatter_rest(work, z, x, along_x, along_z, r1, p1, r2, tr, cps, hook)
    if k == 0:
        grad = fresh
    else:
        gg, image_gram, mix, step = found
        conj = fresh if k == 1 else fresh + exact(mix, conj_in[...], 0, 0)
        grad = grad_in[...] - exact(step, conj, 0, 0)
        conj_out[...] = conj
        state_out[GG] = gg
        state_out[IG] = image_gram
        state_out[MIX1] = mix if k == 2 else jnp.zeros((N, N), F32)
        state_out[STEP0] = step if k == 1 else state_in[STEP0]
        state_out[STEP1] = step if k == 2 else jnp.zeros((N, N), F32)
    for h in range(2):
        for j in range(4):
            at = (4 * h + j) * B
            vec[z, x, h, j] = grad[:, at : at + B]
    grad_out[...] = grad
    tile_out[...] = jnp.zeros_like(tile_out)
    tile_out[:, 0:N] = exact(grad, grad, 1, 1)
    gather_all(place, z, x, along_x, along_z, tr, RS_SLOTS)
    tr.finish()


def exchange(k, n_row, n_col, sums, more):
    shape = (4, n_row // 4, 2, CBD // 2, N, B)
    vmem = pl.BlockSpec(memory_space=pltpu.VMEM)
    width = CBD * B
    outs = [
        jax.ShapeDtypeStruct(shape, F32),
        jax.ShapeDtypeStruct((N, width), F32),
        jax.ShapeDtypeStruct((N, B), F32),
    ]
    slots = RS_SLOTS + AG_SLOTS
    scratch = [
        pltpu.VMEM((2, 4, 6, 2, N, B), F32),
        pltpu.VMEM((2, 4, 4, N, B), F32),
        pltpu.VMEM((2, 6, 2, N, B), F32),
    ]
    boxes = []
    if k:
        outs += [jax.ShapeDtypeStruct((N, width), F32), jax.ShapeDtypeStruct((5, N, N), F32)]
        slots += n_row - 1 + n_col - 1
        boxes = [pltpu.VMEM((n_col, N, B), F32), pltpu.VMEM((n_row, N, B), F32)]
    return pl.pallas_call(
        functools.partial(exchange_kernel, k, n_row, n_col),
        out_shape=outs,
        in_specs=[vmem] * (1 + len(more)),
        out_specs=[vmem] * len(outs),
        scratch_shapes=scratch
        + [pltpu.SemaphoreType.DMA((slots,)), pltpu.SemaphoreType.DMA((slots,))]
        + boxes,
        compiler_params=pltpu.CompilerParams(
            collective_id=k, has_side_effects=True, vmem_limit_bytes=48 * MIB
        ),
    )(sums.reshape(shape), *more)


def coefficient_kernel(n_row, n_col, gram_in, tile_in, state_in, coef, send_sem, recv_sem, box1, box2):
    row, col, z, x, along_x, along_z = places(n_row // 4)
    tr = Traffic(send_sem, recv_sem)
    meet(row, col, n_row, n_col, along_x, along_z, True)
    grams = GramSum(row, col, n_row, n_col, tr, 0, box1, box2)
    grams.first(gram_in[...] + tile_in[...])
    grams.second()
    total = grams.total()
    _, _, mix2, step2 = small_solves(3, total, state_in)
    e1 = state_in[STEP1] + exact(mix2, step2)
    coef[0:N, :] = state_in[STEP0] + exact(state_in[MIX1], e1)
    coef[N : 2 * N, :] = e1
    coef[2 * N : 3 * N, :] = step2
    tr.finish()


def coefficients(n_row, n_col, gram, tile, state):
    vmem = pl.BlockSpec(memory_space=pltpu.VMEM)
    slots = n_row + n_col - 2
    return pl.pallas_call(
        functools.partial(coefficient_kernel, n_row, n_col),
        out_shape=jax.ShapeDtypeStruct((3 * N, N), F32),
        in_specs=[vmem] * 3,
        out_specs=vmem,
        scratch_shapes=[
            pltpu.SemaphoreType.DMA((slots,)),
            pltpu.SemaphoreType.DMA((slots,)),
            pltpu.VMEM((n_col, N, B), F32),
            pltpu.VMEM((n_row, N, B), F32),
        ],
        compiler_params=pltpu.CompilerParams(collective_id=3, has_side_effects=True),
    )(gram, tile, state)


def final_kernel(coef, t, i0, i1, i2, g0, g1, g2, sol, res):
    weights = coef[...]

    @pl.when(pl.program_id(0) == 0)
    def _():
        sol[...] = exact(weights, jnp.concatenate([g0[...], g1[...], g2[...]], axis=0), 0, 0)

    res[...] = t[...] - exact(weights, jnp.concatenate([i0[...], i1[...], i2[...]], axis=0), 0, 0)


def finish(coef, targets, images, grads):
    width = 1024
    strip = pl.BlockSpec((N, width), lambda s: (0, s))
    fixed = pl.BlockSpec((N, CBD * B), lambda s: (0, 0))
    return pl.pallas_call(
        final_kernel,
        grid=(targets.shape[1] // width,),
        out_shape=[
            jax.ShapeDtypeStruct((N, CBD * B), F32),
            jax.ShapeDtypeStruct(targets.shape, F32),
        ],
        in_specs=[pl.BlockSpec((3 * N, N), lambda s: (0, 0))] + [strip] * 4 + [fixed] * 3,
        out_specs=[fixed, strip],
    )(coef, targets, *images, *grads)


def body(blocks, block_cols, targets):
    n_row = lax.axis_size("row")
    n_col = lax.axis_size("col")
    group = CBD * n_row
    flat = block_cols.reshape(-1)
    cols = flat // (CBD * n_col) * CBD + lax.rem(flat, CBD)

    (sums,) = local_pass(False, True, cols, blocks, targets, [], group)
    vec, grad, tile = exchange(0, n_row, n_col, sums, [])
    grads, images = [grad], []
    state = jnp.zeros((5, N, N), F32)
    conj = None
    for k in range(1, ITERS + 1):
        last = k == ITERS
        made = local_pass(True, not last, cols, blocks, vec.reshape(group, N, B), images[::-1], group)
        images.append(made[0])
        gram = made[1]
        if last:
            coef = coefficients(n_row, n_col, gram, tile, state)
        else:
            more = [gram, tile, grad, state] + ([conj] if k >= 2 else [])
            vec, grad, tile, conj, state = exchange(k, n_row, n_col, made[2], more)
            grads.append(grad)
    return tuple(finish(coef, targets, images, grads))


def solution(mesh):
    placed = (P(("row", "col"), None, None, None), P(("row", "col"), None), P(None, ("row", "col")))
    return jax.shard_map(
        body,
        mesh=mesh,
        in_specs=placed,
        out_specs=(P(None, ("row", "col")), P(None, ("row", "col"))),
        check_vma=False,
    )
```

time: 837 us -> 258 us (0.31)
  blocking collectives: 264 us -> 0 us
  Pallas kernels: 0 us -> 251 us
  waiting for transfers between devices: 245 us -> 0 us
  matrix products: 137 us -> 0 us
  other arithmetic: 134 us -> 0.01 us
  local copies, waits for them, and re-layouts: 33.8 us -> 5.68 us
  between operations: 14.7 us -> 0.81 us
    psum x6 -> x0, blocking collectives: 264 us -> none  [the longest x3 197 us: body(): image_gram = lax.psum(gram_of(image), ('row', 'col'))]
    pallas_call x0 -> x9, Pallas kernels: none -> 251 us  [the longest x3 128 us: exchange(): pl.pallas_call(functools.partial(exchange_kernel, k, n_row, n_col), out_s...]
    psum x3 -> x0, waiting for transfers between devices: 245 us -> none  [gradient_of(): gradient = lax.psum(backward(resid), 'row')]
    dot_general x20 -> x0, matrix products: 135 us -> none  [the longest x3 58.2 us: body(): jnp.einsum('ikab,nikb->nia', blocks, picked, precision=lax.Precision.HIGH...]
    scatter-add x3 -> x0, other arithmetic: 90.6 us -> none  [backward(): jax.ops.segment_sum(pieces_all, local_cols, num_segments=group_size)]
    another operation x25 -> x0, other arithmetic: 33.4 us -> none  [the longest x15 18 us: chol_solve(): lower_factor = jnp.linalg.cholesky(matrix)]
    reshape x8 -> x1, local copies, waits for them, and re-layouts: 11.6 us -> 0.1 us  [body(): flat = block_cols.reshape(-1)]
    gather x3 -> x0, local copies, waits for them, and re-layouts: 10.3 us -> none  [body(): jnp.take(tiles, local_cols, axis=1)]
  transfers between devices with their start and end apart: 3 -> 0, of which waited for: 3 -> 0; matrix products, arithmetic and copies ran while one was open for 3% -> 0% of each run, Pallas kernels for 0% -> 0%
where the time goes in v1:
time: 258 us; the launch traced here: 257 us
  Pallas kernels  251 us (97%)
  local copies, waits for them, and re-layouts  5.68 us (2%)
    pallas_call x3, Pallas kernels, exchange(): pl.pallas_call(functools.partial(exchange_kernel, k, n_row, n_col), out_s...  128 us
    pallas_call x4, Pallas kernels, local_pass(): pl.pallas_call(functools.partial(local_kernel, forward, backward, len(bef...  87 us
    pallas_call x1, Pallas kernels, coefficients(): pl.pallas_call(functools.partial(coefficient_kernel, n_row, n_col), out_s...  28.2 us
    pallas_call x1, Pallas kernels, finish(): pl.pallas_call(final_kernel, grid=(targets.shape[1] // width,), out_shape...  7.81 us
    unnamed x23, local copies, waits for them, and re-layouts  5.57 us

profile of v1, /device:TPU:1, one launch (start us, length us, event | category | flops | bytes accessed | tf_op | source)
XLA Modules:
  0.0 257.1 jit_solution(6894280152709317633)
XLA Ops:
  0.6 0.8 copy.5
  1.4 0.1 reshape.25
  1.5 0.0 copy-start.1
  1.5 1.2 copy-done.1
  2.8 10.2 %shard_map.50 = f32[128,32,128]{2,1,0:T(8,128)S(1)} custom-call(s32[256]{0:T(256)S(1)} %fusion.cols, f32[64,4,128,128]{3,2,1,0:T(8,128)} %refs_0_.7, f32[32,8192]{1,0:T(8,128)S(1)} %copy-done.1), custom_call_target="tpu_custom_call" | custom-call | tf_op jit(solution)/shard_map/pallas_call | solution.py:119
  13.0 36.4 %shard_map.51 = (f32[4,4,2,4,32,128]{5,4,3,2,1,0:T(8,128)S(1)}, f32[32,1024]{1,0:T(8,128)S(1)}, f32[32,128]{1,0:T(8,128)S(1)}) custom-call(f32[4,4,2,4,32,128]{5,4,3,2,1,0:T(8,128)S(1)} %bitcast.6), custom_call_target="tpu_custom_call" | custom-call | tf_op jit(solution)/shard_map/pallas_call | solution.py:459
  49.4 0.0 copy-start.5
  49.4 27.0 %shard_map.52 = (f32[32,8192]{1,0:T(8,128)S(1)}, f32[32,128]{1,0:T(8,128)S(1)}, f32[128,32,128]{2,1,0:T(8,128)S(1)}) custom-call(s32[256]{0:T(256)S(1)} %fusion.cols, f32[64,4,128,128]{3,2,1,0:T(8,128)} %refs_0_.7, f32[128,32,128]{2,1,0:T(8,128)S(1)} %bitcast.8), custom_call_target="tpu_custom_call" | custom-call | tf_op jit(solution)/shard_map/pallas_call | solution.py:119
  76.4 0.0 copy-start
  76.5 0.0 copy-done.5
  76.5 44.1 %shard_map.53 = (f32[4,4,2,4,32,128]{5,4,3,2,1,0:T(8,128)S(1)}, f32[32,1024]{1,0:T(8,128)S(1)}, f32[32,128]{1,0:T(8,128)S(1)}, f32[32,1024]{1,0:T(8,128)S(1)}, f32[5,32,32]{2,1,0:T(8,128)S(1)}) custom-call(f32[4,4,2,4,32,128]{5,4,3,2,1,0:T(8,128)S(1)} %bitcast.9, f32[32,128]{1,0:T(8,128)S(1)} %get-tuple-element.24.refs_1_, ...), custom_call_target="tpu_custom_call" | custom-call | tf_op jit(solution)/shard_map/pallas_call | solution.py:459
  120.6 0.0 copy-start.3
  120.6 1.3 copy-done.3
  121.9 0.0 copy-start.6
  121.9 25.4 %shard_map.54 = (f32[32,8192]{1,0:T(8,128)S(1)}, f32[32,128]{1,0:T(8,128)S(1)}, f32[128,32,128]{2,1,0:T(8,128)S(1)}) custom-call(s32[256]{0:T(256)S(1)} %fusion.cols, f32[64,4,128,128]{3,2,1,0:T(8,128)} %refs_0_.7, f32[128,32,128]{2,1,0:T(8,128)} %bitcast.7, f32[32,8192]{1,0:T(8,128)S(1)} %get-tuple-element.28.refs_2_.refs_3_.i0), custom_call_target="tpu_custom_call" | custom-call | tf_op jit(solution)/shard_map/pallas_call | solution.py:119
  147.3 0.0 copy-start.2
  147.3 0.0 copy-done.6
  147.4 47.0 %shard_map.55 = (f32[4,4,2,4,32,128]{5,4,3,2,1,0:T(8,128)S(1)}, f32[32,1024]{1,0:T(8,128)S(1)}, f32[32,128]{1,0:T(8,128)S(1)}, f32[32,1024]{1,0:T(8,128)}, f32[5,32,32]{2,1,0:T(8,128)S(1)}) custom-call(f32[4,4,2,4,32,128]{5,4,3,2,1,0:T(8,128)S(1)} %bitcast.10, f32[32,128]{1,0:T(8,128)S(1)} %get-tuple-element.30.refs_1_, ...), custom_call_target="tpu_custom_call" | custom-call | tf_op jit(solution)/shard_map/pallas_call | solution.py:459
  194.4 0.0 copy-start.7
  194.4 0.6 copy-done.7
  195.1 0.0 copy-start.8
  195.1 0.0 copy-start.9
  195.1 0.0 copy-done
  195.1 24.3 %shard_map.56 = (f32[32,8192]{1,0:T(8,128)S(1)}, f32[32,128]{1,0:T(8,128)S(1)}) custom-call(s32[256]{0:T(256)S(1)} %fusion.cols, f32[64,4,128,128]{3,2,1,0:T(8,128)} %refs_0_.7, f32[128,32,128]{2,1,0:T(8,128)S(1)} %bitcast.11, f32[32,8192]{1,0:T(8,128)S(1)} %get-tuple-element.36.refs_2_.i1, f32[32,8192]{1,0:T(8,128)S(1)} %get-tuple-element.28.refs_2_.refs_3_.i0), custom_call_target="tpu_custom_call" | custom-call | tf_op jit(solution)/shard_map/pallas_call | solution.py:119
  219.4 0.0 copy-done.2
  219.4 0.0 copy-done.8
  219.4 0.0 copy-done.9
  219.4 0.0 copy-start.4
  219.4 1.0 copy-done.4
  220.4 0.6 copy-done.10
  221.0 28.2 %shard_map.57.coef = f32[96,32]{1,0:T(8,128)} custom-call(f32[32,128]{1,0:T(8,128)} %copy-done.10, f32[32,128]{1,0:T(8,128)} %copy-done.9, f32[5,32,32]{2,1,0:T(8,128)} %copy-done.8), custom_call_target="tpu_custom_call" | custom-call | tf_op jit(solution)/shard_map/pallas_call | solution.py:492
  249.3 7.8 %shard_map.58 = (f32[32,1024]{1,0:T(8,128)}, f32[32,8192]{1,0:T(8,128)}) custom-call(f32[96,32]{1,0:T(8,128)} %shard_map.57.coef, f32[32,8192]{1,0:T(8,128)} %t.1, f32[32,8192]{1,0:T(8,128)} %copy-done, f32[32,8192]{1,0:T(8,128)} %copy-done.2, f32[32,8192]{1,0:T(8,128)} %copy-done.4, f32[32,1024]{1,0:T(8,128)} %copy-done.5, f32[32,1024]{1,0:T(8,128)} %copy-done.6, ...), custom_call_target="tpu_custom_call" | custom-call | tf_op jit(solution)/shard_map/pallas_call | solution.py:521
  (3 shorter events, 0.0 us)
Async XLA Ops:
  1.5 1.2 copy-start.1
  49.4 27.1 %copy-start.5 = (f32[32,1024]{1,0:T(8,128)}, f32[32,1024]{1,0:T(8,128)S(1)}, u32[]{:S(2)}) copy-start(f32[32,1024]{1,0:T(8,128)S(1)} %get-tuple-element.26.refs_3_.g0) | copy-start | bytes 393220
  76.4 118.6 %copy-start = (f32[32,8192]{1,0:T(8,128)}, f32[32,8192]{1,0:T(8,128)S(1)}, u32[]{:S(2)}) copy-start(f32[32,8192]{1,0:T(8,128)S(1)} %get-tuple-element.28.refs_2_.refs_3_.i0) | copy-start | bytes 3145732
  120.6 1.3 copy-start.3
  121.9 25.4 %copy-start.6 = (f32[32,1024]{1,0:T(8,128)}, f32[32,1024]{1,0:T(8,128)S(1)}, u32[]{:S(2)}) copy-start(f32[32,1024]{1,0:T(8,128)S(1)} %get-tuple-element.32.refs_3_.g1) | copy-start | bytes 393220
  147.3 72.1 %copy-start.2 = (f32[32,8192]{1,0:T(8,128)}, f32[32,8192]{1,0:T(8,128)S(1)}, u32[]{:S(2)}) copy-start(f32[32,8192]{1,0:T(8,128)S(1)} %get-tuple-element.36.refs_2_.i1) | copy-start | bytes 3145732
  194.4 0.7 copy-start.7
  195.1 24.3 %copy-start.8 = (f32[5,32,32]{2,1,0:T(8,128)}, f32[5,32,32]{2,1,0:T(8,128)S(1)}, u32[]{:S(2)}) copy-start(f32[5,32,32]{2,1,0:T(8,128)S(1)} %get-tuple-element.39.state_in) | copy-start | bytes 61444
  195.1 24.4 %copy-start.9 = (f32[32,128]{1,0:T(8,128)}, f32[32,128]{1,0:T(8,128)S(1)}, u32[]{:S(2)}) copy-start(f32[32,128]{1,0:T(8,128)S(1)} %get-tuple-element.38.tile_in) | copy-start | bytes 49156
  219.4 1.0 copy-start.4
  220.4 0.6 copy-start.10

commit v2 on v1

v2 whole, which is shorter than its diff:
```python
import functools

import jax
import jax.numpy as jnp
from jax import lax
from jax.experimental import pallas as pl
from jax.experimental.pallas import tpu as pltpu
from jax.sharding import PartitionSpec as P

MESH = pl.DeviceIdType.MESH
F32 = jnp.float32
BF16 = jnp.bfloat16
ITERS = 3
CBD = 8
N = 32
B = 128
STEP_ROWS = 8
MIB = 2**20


def dot(a, b, ca, cb, precision=None):
    return lax.dot_general(
        a, b, (((ca,), (cb,)), ((), ())), precision=precision, preferred_element_type=F32
    )


def exact(a, b, ca=1, cb=0):
    return dot(a, b, ca, cb, lax.Precision.HIGHEST)


def split(x):
    hi = x.astype(BF16)
    lo = (x - hi.astype(F32)).astype(BF16)
    return hi, lo


def stacked(x):
    hi, lo = split(x)
    return jnp.concatenate([hi, lo], axis=0)


def pack(square):
    return jnp.concatenate([square[8 * g : 8 * g + 8] for g in range(4)], axis=1)


def unpack(tile):
    return jnp.concatenate([tile[:, N * g : N * g + N] for g in range(4)], axis=0)


def fold(square):
    half = square[:N] + square[N:]
    return half[:, :N] + half[:, N:]


def add_pieces(cols, base, both, block, sums):
    piece = dot(jnp.concatenate([both, both], axis=1), block, 1, 0)
    piece = piece[:N] + piece[N:]
    for k in range(4):
        c = cols[base + k]
        sums[c] += piece[:, k * B : (k + 1) * B]


def first_kernel(cols, blocks, targets, across_out, down_out, sums):
    step = pl.program_id(0)

    @pl.when(step == 0)
    def _():
        sums[...] = jnp.zeros_like(sums)

    for i in range(STEP_ROWS):
        his, los = [], []
        for k in range(4):
            hi, lo = split(blocks[i, k])
            his.append(hi)
            los.append(lo)
            down_out[i, k * B : (k + 1) * B, 0:B] = hi.T
            down_out[i, k * B : (k + 1) * B, B : 2 * B] = lo.T
        across = jnp.concatenate([jnp.concatenate(his, axis=1), jnp.concatenate(los, axis=1)], axis=0)
        across_out[i] = across
        both = stacked(targets[:, i * B : (i + 1) * B])
        add_pieces(cols, (step * STEP_ROWS + i) * 4, both, across, sums)


def first_pass(cols, blocks, targets, group):
    rows = blocks.shape[0]
    return pl.pallas_call(
        first_kernel,
        grid_spec=pltpu.PrefetchScalarGridSpec(
            num_scalar_prefetch=1,
            grid=(rows // STEP_ROWS,),
            in_specs=[
                pl.BlockSpec((STEP_ROWS, 4, B, B), lambda s, c: (s, 0, 0, 0)),
                pl.BlockSpec((N, STEP_ROWS * B), lambda s, c: (0, s)),
            ],
            out_specs=[
                pl.BlockSpec((STEP_ROWS, 2 * B, 4 * B), lambda s, c: (s, 0, 0)),
                pl.BlockSpec((STEP_ROWS, 4 * B, 2 * B), lambda s, c: (s, 0, 0)),
                pl.BlockSpec((group, N, B), lambda s, c: (0, 0, 0)),
            ],
        ),
        out_shape=[
            jax.ShapeDtypeStruct((rows, 2 * B, 4 * B), BF16),
            jax.ShapeDtypeStruct((rows, 4 * B, 2 * B), BF16),
            jax.ShapeDtypeStruct((group, N, B), F32),
        ],
        compiler_params=pltpu.CompilerParams(vmem_limit_bytes=48 * MIB),
    )(cols, blocks, targets)


def pass_kernel(k, backward, cols, *refs):
    refs = list(refs)
    down = refs.pop(0)
    across = refs.pop(0) if backward else None
    vec = refs.pop(0)
    before = [refs.pop(0) for _ in range(k)]
    state = [refs.pop(0) for _ in range(k)]
    gram_before = refs.pop(0) if k else None
    image_out, gram_out, tile_out = (refs.pop(0) for _ in range(3))
    sums = refs.pop(0) if backward else None
    parts, gram_acc = refs
    step = pl.program_id(0)

    @pl.when(step == 0)
    def _():
        if backward:
            sums[...] = jnp.zeros_like(sums)
        gram_acc[...] = jnp.zeros_like(gram_acc)

        def cut(c, carry):
            parts[c] = stacked(vec[c])
            return carry

        lax.fori_loop(0, vec.shape[0], cut, 0, unroll=8)

    for i in range(STEP_ROWS):
        base = (step * STEP_ROWS + i) * 4
        picked = jnp.concatenate([parts[cols[base + j]] for j in range(4)], axis=1)
        quad = dot(picked, down[i], 1, 0)
        quad = quad[:N] + quad[N:]
        both = stacked(quad[:, :B] + quad[:, B:])
        image_out[:, i * B : (i + 1) * B] = both
        if backward:
            add_pieces(cols, base, both, across[i], sums)
    mine = image_out[...]
    for j, other in enumerate([mine] + [e[...] for e in before]):
        gram_acc[j] += dot(mine, other, 1, 1)

    @pl.when(step == pl.num_programs(0) - 1)
    def _():
        gram = fold(gram_acc[0])
        if k:
            mix = state[0][MIX]
            cross = fold(gram_acc[1])
            if k == 2:
                cross = cross + exact(fold(gram_acc[2]), state[1][MIX])
            mixed = exact(cross, mix)
            gram = gram + (mixed + mixed.T) + exact(mix, exact(gram_before[...], mix), 0, 0)
        gram_out[...] = gram
        tile_out[...] = pack(gram)


def local_pass(k, backward, cols, down, across, vec, images, states, gram, group):
    rows = down.shape[0]
    strip = pl.BlockSpec((2 * N, STEP_ROWS * B), lambda s, c: (0, s))
    whole = pl.BlockSpec((group, N, B), lambda s, c: (0, 0, 0))
    square = pl.BlockSpec((N, N), lambda s, c: (0, 0))
    three = pl.BlockSpec((3, N, N), lambda s, c: (0, 0, 0))
    args = [down] + ([across] if backward else []) + [vec]
    in_specs = [pl.BlockSpec((STEP_ROWS, 4 * B, 2 * B), lambda s, c: (s, 0, 0))]
    if backward:
        in_specs += [pl.BlockSpec((STEP_ROWS, 2 * B, 4 * B), lambda s, c: (s, 0, 0))]
    in_specs += [whole]
    if k:
        args += images[::-1] + states[::-1][:k] + [gram]
        in_specs += [strip] * k + [three] * k + [square]
    outs = [
        jax.ShapeDtypeStruct((2 * N, rows * B), BF16),
        jax.ShapeDtypeStruct((N, N), F32),
        jax.ShapeDtypeStruct((8, B), F32),
    ]
    out_specs = [strip, square, pl.BlockSpec((8, B), lambda s, c: (0, 0))]
    if backward:
        outs += [jax.ShapeDtypeStruct((group, N, B), F32)]
        out_specs += [whole]
    return pl.pallas_call(
        functools.partial(pass_kernel, k, backward),
        grid_spec=pltpu.PrefetchScalarGridSpec(
            num_scalar_prefetch=1,
            grid=(rows // STEP_ROWS,),
            in_specs=in_specs,
            out_specs=out_specs,
            scratch_shapes=[
                pltpu.VMEM((group, 2 * N, B), BF16),
                pltpu.VMEM((k + 1, 2 * N, 2 * N), F32),
            ],
        ),
        out_shape=outs,
        compiler_params=pltpu.CompilerParams(vmem_limit_bytes=48 * MIB),
    )(cols, *args)


def spd_solve(matrix, right):
    table = jnp.concatenate([matrix, right], axis=1)
    wide = (8, 2 * N)
    parts = [table[8 * g : 8 * g + 8] for g in range(4)]
    sub = lax.broadcasted_iota(jnp.int32, wide, 0)

    def lanes(group, b):
        return jnp.broadcast_to(group[:, b : b + 1], wide)

    def rows(group, a):
        return jnp.broadcast_to(group[a : a + 1], wide)

    for g in range(4):
        mine = parts[g]
        pivots = [lanes(mine, 8 * g + b) for b in range(8)]
        factors = [[lanes(parts[h], 8 * g + b) for b in range(8)] if h != g else None for h in range(4)]
        for a in range(8):
            inverse = 1.0 / rows(pivots[a], a)
            here = sub == a
            factor = pivots[a]
            for b in range(a + 1, 8):
                scaled = rows(pivots[b], a) * inverse
                pivots[b] = jnp.where(here, scaled, pivots[b] - factor * scaled)
            scaled = rows(mine, a) * inverse
            mine = jnp.where(here, scaled, mine - factor * scaled)
        parts[g] = mine
        for h in range(4):
            if h != g:
                for b in range(8):
                    parts[h] = parts[h] - factors[h][b] * rows(mine, b)
    return jnp.concatenate(parts, axis=0)[:, N : 2 * N]


def apply_t(square, both):
    hi, lo = split(square.T)
    left = jnp.concatenate([jnp.concatenate([hi, hi], axis=1), jnp.concatenate([lo, lo], axis=1)], axis=0)
    out = dot(left, both, 1, 0)
    return out[:N] + out[N:]


class Traffic:
    def __init__(self, send_sem, recv_sem):
        self.send_sem, self.recv_sem = send_sem, recv_sem
        self.sent = []

    def send(self, slot, src, dst, device):
        copy = pltpu.make_async_remote_copy(
            src_ref=src,
            dst_ref=dst,
            send_sem=self.send_sem.at[slot],
            recv_sem=self.recv_sem.at[slot],
            device_id=device,
            device_id_type=MESH,
        )
        copy.start()
        self.sent.append(copy)
        return copy

    def finish(self):
        for copy in self.sent:
            copy.wait_send()


OFFSETS = (2, 3, 1, 0)


def places(n_x):
    row = lax.axis_index("row")
    col = lax.axis_index("col")
    z, x = row // n_x, lax.rem(row, n_x)

    def along_x(d):
        return (z * n_x + lax.rem(x + d, n_x), col)

    def along_z(d):
        return (lax.rem(z + d, 4) * n_x + x, col)

    return row, col, z, x, along_x, along_z


def reduce_scatter_start(work, z, x, along_x, along_z, r1, tr):
    cps = {}
    for u in range(4):
        for h in range(2):
            pa, pb, ring = (x, z, along_x) if h == 0 else (z, x, along_z)
            tb = lax.rem(pb + OFFSETS[u], 4)

            def src(ta, s, h=h, tb=tb):
                ta = lax.rem(ta, 4)
                return work(h, ta, tb, s)

            base = (h * 4 + u) * 6
            for idx, ta, s, d in ((0, pa + 2, 0, 1), (1, pa + 2, 1, 3), (2, pa + 1, 1, 1), (3, pa + 3, 0, 3)):
                cps[h, u, idx] = tr.send(base + idx, src(ta, s), r1.at[h, u, idx], ring(d))
    return cps


def reduce_scatter_rest(work, z, x, along_x, along_z, r1, p1, r2, tr, cps, hook):
    c2 = {}
    halves = ((x, z, along_x, along_z), (z, x, along_z, along_x))

    def pass_on(u, h):
        pa, pb, ring, _ = halves[h]
        tb = lax.rem(pb + OFFSETS[u], 4)
        base = (h * 4 + u) * 6
        cps[h, u, 0].wait_recv()
        r1[h, u, 0] += work(h, lax.rem(pa + 1, 4), tb, 0)[...]
        cps[h, u, 4] = tr.send(base + 4, r1.at[h, u, 0], r1.at[h, u, 4], ring(1))
        cps[h, u, 1].wait_recv()
        r1[h, u, 1] += work(h, lax.rem(pa + 3, 4), tb, 1)[...]
        cps[h, u, 5] = tr.send(base + 5, r1.at[h, u, 1], r1.at[h, u, 5], ring(3))

    def close(u, h):
        pa, pb, _, ring = halves[h]
        tb = lax.rem(pb + OFFSETS[u], 4)
        base = 48 + h * 6
        for idx in (2, 3, 4, 5):
            cps[h, u, idx].wait_recv()
        p1[h, u, 0:2] = work(h, pa, tb, 0)[...] + (r1[h, u, 3] + r1[h, u, 4])
        p1[h, u, 2:4] = work(h, pa, tb, 1)[...] + (r1[h, u, 2] + r1[h, u, 5])
        if u == 0:
            c2[h, 0] = tr.send(base + 0, p1.at[h, 0, pl.ds(0, 2)], r2.at[h, 0], ring(1))
            c2[h, 1] = tr.send(base + 1, p1.at[h, 0, pl.ds(2, 2)], r2.at[h, 1], ring(3))
        if u == 1:
            c2[h, 3] = tr.send(base + 3, p1.at[h, 1, pl.ds(0, 2)], r2.at[h, 3], ring(3))
            c2[h, 1].wait_recv()
            r2[h, 1] += p1[h, 1, 2:4]
            c2[h, 5] = tr.send(base + 5, r2.at[h, 1], r2.at[h, 5], ring(3))
        if u == 2:
            c2[h, 2] = tr.send(base + 2, p1.at[h, 2, pl.ds(2, 2)], r2.at[h, 2], ring(1))
            c2[h, 0].wait_recv()
            r2[h, 0] += p1[h, 2, 0:2]
            c2[h, 4] = tr.send(base + 4, r2.at[h, 0], r2.at[h, 4], ring(1))

    for u in range(5):
        if u < 4:
            for h in range(2):
                pass_on(u, h)
        if u >= 1:
            for h in range(2):
                close(u - 1, h)
        hook(u)
    own = []
    for h in range(2):
        for idx in (2, 3, 4, 5):
            c2[h, idx].wait_recv()
        first = p1[h, 3, 0:2] + (r2[h, 3] + r2[h, 4])
        second = p1[h, 3, 2:4] + (r2[h, 2] + r2[h, 5])
        own += [first[0], first[1], second[0], second[1]]
    return jnp.concatenate(own, axis=1)


def gather_all(place, z, x, along_x, along_z, tr, base0, hook):
    halves = ((x, z, along_x, along_z), (z, x, along_z, along_x))
    c1, c2 = {}, {}
    order = (0, 3, 1, 2)

    def send1(h, idx):
        pa, pb, _, ring = halves[h]
        off, s, d = ((0, None, 1), (0, None, 3), (3, 0, 1), (1, 1, 3))[idx]
        ref = place(h, pa, lax.rem(pb + off, 4), s)
        c1[h, idx] = tr.send(base0 + h * 4 + idx, ref, ref, ring(d))

    def send2(h, v, idx):
        pa, pb, ring, _ = halves[h]
        tb = lax.rem(pb + order[v], 4)
        off, s, d = ((0, None, 1), (0, None, 3), (3, 0, 1), (1, 1, 3))[idx]
        ref = place(h, lax.rem(pa + off, 4), tb, s)
        c2[h, v, idx] = tr.send(base0 + 8 + (h * 4 + v) * 4 + idx, ref, ref, ring(d))

    both = range(2)
    for h in both:
        send1(h, 0)
        send1(h, 1)
    for h in both:
        send2(h, 0, 0)
        send2(h, 0, 1)
    for h in both:
        c1[h, 0].wait_recv()
        send1(h, 2)
        send2(h, 1, 0)
        send2(h, 1, 1)
        c1[h, 1].wait_recv()
        send1(h, 3)
        send2(h, 2, 0)
        send2(h, 2, 1)
    for v in range(4):
        for h in both:
            if v == 1:
                c1[h, 2].wait_recv()
                c1[h, 3].wait_recv()
                send2(h, 3, 0)
                send2(h, 3, 1)
            c2[h, v, 0].wait_recv()
            send2(h, v, 2)
            c2[h, v, 1].wait_recv()
            send2(h, v, 3)
        hook(v)
    for v in range(4):
        for h in both:
            c2[h, v, 2].wait_recv()
            c2[h, v, 3].wait_recv()


RS_SLOTS = 60
AG_SLOTS = 40


SUM_SLOTS = 10


def sum_stages(row, col, n_row, n_col):
    n_x, n_y = n_row // 4, n_col // 2
    z, x = row // n_x, lax.rem(row, n_x)
    y, core = col // 2, lax.rem(col, 2)
    return [
        ([(row, y * 2 + 1 - core)], core, 2),
        ([(row, lax.rem(y + d, n_y) * 2 + core) for d in range(1, n_y)], y, n_y),
        ([(z * n_x + lax.rem(x + d, n_x), col) for d in range(1, n_x)], x, n_x),
        ([(lax.rem(z + d, 4) * n_x + x, col) for d in range(1, 4)], z, 4),
    ]


class TileSum:
    def __init__(self, stages, tr, slot, box):
        self.stages, self.tr, self.slot, self.box = stages, tr, slot, box
        self.at, self.open = 0, []

    def put(self, tile):
        peers, me, _ = self.stages[self.at]
        ref = self.box.at[self.at, me]
        self.box[self.at, me] = tile
        self.open = []
        for device in peers:
            self.open.append(self.tr.send(self.slot, ref, ref, device))
            self.slot += 1

    def take(self):
        for c in self.open:
            c.wait_recv()
        size = self.stages[self.at][2]
        total = self.box[self.at, 0]
        for i in range(1, size):
            total = total + self.box[self.at, i]
        self.at += 1
        return total

    def step(self):
        self.put(self.take())


def meet(stages):
    barrier = pltpu.get_barrier_semaphore()
    who = [device for peers, _, _ in stages for device in peers]
    for device in who:
        pl.semaphore_signal(barrier, inc=1, device_id=device, device_id_type=MESH)
    pl.semaphore_wait(barrier, len(who))


GG, MIX, STEP = range(3)


def exchange_kernel(k, n_row, n_col, *refs):
    refs = list(refs)
    sums = refs.pop(0)
    if k:
        tile_in, grad_in, state_in = (refs.pop(0) for _ in range(3))
    conj_in = refs.pop(0) if k >= 2 else None
    vec, grad_out, state_out = (refs.pop(0) for _ in range(3))
    conj_out = refs.pop(0) if k else None
    r1, p1, r2, box, send_sem, recv_sem = refs
    row, col, z, x, along_x, along_z = places(n_row // 4)
    stages = sum_stages(row, col, n_row, n_col)
    tr = Traffic(send_sem, recv_sem)
    meet(stages)

    def work(h, ta, tb, s):
        zz, xx = (tb, ta) if h == 0 else (ta, tb)
        return sums.at[zz, xx, h, pl.ds(2 * s, 2)]

    def place(h, ta, tb, s):
        zz, xx = (tb, ta) if h == 0 else (ta, tb)
        return vec.at[zz, xx, h] if s is None else vec.at[zz, xx, h, pl.ds(2 * s, 2)]

    slots = RS_SLOTS + AG_SLOTS
    if k:
        image_sum = TileSum(stages, tr, slots, box.at[0])
        image_sum.put(tile_in[...])
    cps = reduce_scatter_start(work, z, x, along_x, along_z, r1, tr)
    found = []

    def beside_first(u):
        if k and u < 3:
            image_sum.step()
        if k and u == 3:
            found.append(spd_solve(unpack(image_sum.take()), state_in[GG]))

    fresh = reduce_scatter_rest(work, z, x, along_x, along_z, r1, p1, r2, tr, cps, beside_first)
    if k == 0:
        grad = fresh
    else:
        (step,) = found
        conj = fresh if k == 1 else fresh + apply_t(state_in[MIX], stacked(conj_in[...]))
        grad = grad_in[...] - apply_t(step, stacked(conj))
    for h in range(2):
        for j in range(4):
            at = (4 * h + j) * B
            vec[z, x, h, j] = grad[:, at : at + B]
    grad_sum = TileSum(stages, tr, slots + SUM_SLOTS, box.at[1])

    def beside_second(v):
        if v == 0:
            both = stacked(grad)
            grad_sum.put(pack(fold(dot(both, both, 1, 1))))
            grad_out[...] = grad
            if k:
                conj_out[...] = conj
        else:
            grad_sum.step()

    gather_all(place, z, x, along_x, along_z, tr, RS_SLOTS, beside_second)
    gram = unpack(grad_sum.take())
    state_out[GG] = gram
    state_out[MIX] = spd_solve(state_in[GG], gram) if k else jnp.zeros((N, N), F32)
    state_out[STEP] = step if k else jnp.zeros((N, N), F32)
    tr.finish()


def exchange(k, n_row, n_col, sums, more):
    shape = (4, n_row // 4, 2, CBD // 2, N, B)
    vmem = pl.BlockSpec(memory_space=pltpu.VMEM)
    width = CBD * B
    outs = [
        jax.ShapeDtypeStruct(shape, F32),
        jax.ShapeDtypeStruct((N, width), F32),
        jax.ShapeDtypeStruct((3, N, N), F32),
    ]
    if k:
        outs += [jax.ShapeDtypeStruct((N, width), F32)]
    slots = RS_SLOTS + AG_SLOTS + 2 * SUM_SLOTS
    return pl.pallas_call(
        functools.partial(exchange_kernel, k, n_row, n_col),
        out_shape=outs,
        in_specs=[vmem] * (1 + len(more)),
        out_specs=[vmem] * len(outs),
        scratch_shapes=[
            pltpu.VMEM((2, 4, 6, 2, N, B), F32),
            pltpu.VMEM((2, 4, 4, N, B), F32),
            pltpu.VMEM((2, 6, 2, N, B), F32),
            pltpu.VMEM((2, 4, 4, 8, B), F32),
            pltpu.SemaphoreType.DMA((slots,)),
            pltpu.SemaphoreType.DMA((slots,)),
        ],
        compiler_params=pltpu.CompilerParams(
            collective_id=k, has_side_effects=True, vmem_limit_bytes=48 * MIB
        ),
    )(sums.reshape(shape), *more)


def last_kernel(n_row, n_col, *refs):
    tile_in, s1, s2, t_hbm, i0, i1, i2, g0, g1, g2, sol, res = refs[:12]
    t_mem, i_mem, g_mem, box, send_sem, recv_sem, load_sem = refs[12:]
    loads = [pltpu.make_async_copy(t_hbm, t_mem, load_sem.at[0])]
    for j, (image, grad) in enumerate(((i0, g0), (i1, g1), (i2, g2))):
        loads.append(pltpu.make_async_copy(image, i_mem.at[pl.ds(2 * N * j, 2 * N)], load_sem.at[1 + 2 * j]))
        loads.append(pltpu.make_async_copy(grad, g_mem.at[j], load_sem.at[2 + 2 * j]))
    for copy in loads:
        copy.start()
    row, col = lax.axis_index("row"), lax.axis_index("col")
    stages = sum_stages(row, col, n_row, n_col)
    tr = Traffic(send_sem, recv_sem)
    meet(stages)
    image_sum = TileSum(stages, tr, 0, box)
    image_sum.put(tile_in[...])
    for _ in range(3):
        image_sum.step()
    total = image_sum.take()
    e2 = spd_solve(unpack(total), s2[GG])
    e1 = s2[STEP] + exact(s2[MIX], e2)
    e0 = s1[STEP] + exact(s1[MIX], e1)
    his, los = [], []
    for e in (e0, e1, e2):
        hi, lo = split(e.T)
        his += [hi, hi]
        los += [lo, lo]
    left = jnp.concatenate([jnp.concatenate(his, axis=1), jnp.concatenate(los, axis=1)], axis=0)
    for copy in loads:
        copy.wait()
    right = jnp.concatenate([stacked(g_mem[j]) for j in range(3)], axis=0)
    out = dot(left, right, 1, 0)
    sol[...] = out[:N] + out[N:]
    width = 1024

    def strip(s, carry):
        at = pl.ds(pl.multiple_of(s * width, width), width)
        out = dot(left, i_mem[:, at], 1, 0)
        res[:, at] = t_mem[:, at] - (out[:N] + out[N:])
        return carry

    lax.fori_loop(0, t_mem.shape[1] // width, strip, 0)
    tr.finish()


def last(n_row, n_col, tile, states, targets, images, grads):
    vmem = pl.BlockSpec(memory_space=pltpu.VMEM)
    anywhere = pl.BlockSpec(memory_space=pl.ANY)
    width = CBD * B
    return pl.pallas_call(
        functools.partial(last_kernel, n_row, n_col),
        out_shape=[jax.ShapeDtypeStruct((N, width), F32), jax.ShapeDtypeStruct(targets.shape, F32)],
        in_specs=[vmem] * 3 + [anywhere] * 7,
        out_specs=[vmem] * 2,
        scratch_shapes=[
            pltpu.VMEM(targets.shape, F32),
            pltpu.VMEM((6 * N, targets.shape[1]), BF16),
            pltpu.VMEM((3, N, width), F32),
            pltpu.VMEM((4, 4, 8, B), F32),
            pltpu.SemaphoreType.DMA((SUM_SLOTS,)),
            pltpu.SemaphoreType.DMA((SUM_SLOTS,)),
            pltpu.SemaphoreType.DMA((7,)),
        ],
        compiler_params=pltpu.CompilerParams(
            collective_id=3, has_side_effects=True, vmem_limit_bytes=32 * MIB
        ),
    )(tile, *states, targets, *images, *grads)


def body(blocks, block_cols, targets):
    n_row = lax.axis_size("row")
    n_col = lax.axis_size("col")
    group = CBD * n_row
    flat = block_cols.reshape(-1)
    cols = flat // (CBD * n_col) * CBD + lax.rem(flat, CBD)

    across, down, sums = first_pass(cols, blocks, targets, group)
    vec, grad, state = exchange(0, n_row, n_col, sums, [])
    grads, images, states = [grad], [], [state]
    conj = gram = None
    for k in range(ITERS):
        final = k + 1 == ITERS
        made = local_pass(
            k, not final, cols, down, across, vec.reshape(group, N, B), images, states, gram, group
        )
        images.append(made[0])
        gram, tile = made[1], made[2]
        if not final:
            more = [tile, grad, state] + ([conj] if k else [])
            vec, grad, state, conj = exchange(k + 1, n_row, n_col, made[3], more)
            grads.append(grad)
            states.append(state)
    return tuple(last(n_row, n_col, tile, states[1:], targets, images, grads))


def solution(mesh):
    placed = (P(("row", "col"), None, None, None), P(("row", "col"), None), P(None, ("row", "col")))
    return jax.shard_map(
        body,
        mesh=mesh,
        in_specs=placed,
        out_specs=(P(None, ("row", "col")), P(None, ("row", "col"))),
        check_vma=False,
    )
```

time: 258 us -> 219 us (0.85)
  Pallas kernels: 251 us -> 212 us
    pallas_call x6 -> x5, Pallas kernels: 123 us -> 84.1 us  [the longest x3 45.4 us: local_pass(): pl.pallas_call(functools.partial(pass_kernel, k, backward), grid_spec=plt...]
    unnamed x23 -> x9, local copies, waits for them, and re-layouts: 5.57 us -> 4.96 us
where the time goes in v2:
time: 219 us; the launch traced here: 218 us
  Pallas kernels  212 us (97%)
  local copies, waits for them, and re-layouts  5.06 us (2%)
    pallas_call x3, Pallas kernels, exchange(): pl.pallas_call(functools.partial(exchange_kernel, k, n_row, n_col), out_s...  128 us
    pallas_call x3, Pallas kernels, local_pass(): pl.pallas_call(functools.partial(pass_kernel, k, backward), grid_spec=plt...  45.4 us
    pallas_call x1, Pallas kernels, first_pass(): pl.pallas_call(first_kernel, grid_spec=pltpu.PrefetchScalarGridSpec(num_s...  19.5 us
    pallas_call x1, Pallas kernels, last(): pl.pallas_call(functools.partial(last_kernel, n_row, n_col), out_shape=[j...  19.2 us
    unnamed x9, local copies, waits for them, and re-layouts  4.96 us

profile of v2, /device:TPU:1, one launch (start us, length us, event | category | flops | bytes accessed | tf_op | source)
XLA Modules:
  0.0 217.6 jit_solution(3067266774567712028)
XLA Ops:
  0.6 0.8 copy.5
  1.4 0.1 reshape.25
  1.5 0.0 copy-start
  1.5 1.2 copy-done
  2.8 19.5 %shard_map.50 = (bf16[64,256,512]{2,1,0:T(8,128)(2,1)}, bf16[64,512,256]{2,1,0:T(8,128)(2,1)}, f32[128,32,128]{2,1,0:T(8,128)S(1)}) custom-call(s32[256]{0:T(256)S(1)} %fusion.cols, f32[64,4,128,128]{3,2,1,0:T(8,128)} %blocks.1, f32[32,8192]{1,0:T(8,128)S(1)} %copy-done), custom_call_target="tpu_custom_call" | custom-call | tf_op jit(solution)/shard_map/pallas_call | solution.py:86
  22.3 42.4 %shard_map.51 = (f32[4,4,2,4,32,128]{5,4,3,2,1,0:T(8,128)S(1)}, f32[32,1024]{1,0:T(8,128)S(1)}, f32[3,32,32]{2,1,0:T(8,128)S(1)}) custom-call(f32[4,4,2,4,32,128]{5,4,3,2,1,0:T(8,128)S(1)} %bitcast.10), custom_call_target="tpu_custom_call" | custom-call | tf_op jit(solution)/shard_map/pallas_call | solution.py:542
  64.7 15.8 %shard_map.52 = (bf16[64,8192]{1,0:T(8,128)(2,1)S(1)}, f32[32,32]{1,0:T(8,128)S(1)}, f32[8,128]{1,0:T(8,128)S(1)}, f32[128,32,128]{2,1,0:T(8,128)S(1)}) custom-call(s32[256]{0:T(256)S(1)} %fusion.cols, bf16[64,512,256]{2,1,0:T(8,128)(2,1)} %get-tuple-element.25.refs_0_, bf16[64,256,512]{2,1,0:T(8,128)(2,1)} %get-tuple-element.26.refs_1_, ...), custom_call_target="tpu_custom_call" | custom-call | tf_op jit(solution)/shard_map/pallas_call | solution.py:185
  80.5 42.1 %shard_map.53 = (f32[4,4,2,4,32,128]{5,4,3,2,1,0:T(8,128)S(1)}, f32[32,1024]{1,0:T(8,128)S(1)}, f32[3,32,32]{2,1,0:T(8,128)S(1)}, f32[32,1024]{1,0:T(8,128)S(1)}) custom-call(f32[4,4,2,4,32,128]{5,4,3,2,1,0:T(8,128)S(1)} %bitcast.9, f32[8,128]{1,0:T(8,128)S(1)} %get-tuple-element.30.refs_1_, f32[32,1024]{1,0:T(8,128)S(1)} %get-tuple-element.31.refs_2_.refs_7_, ...), custom_call_target="tpu_custom_call" | custom-call | tf_op jit(solution)/shard_map/pallas_call | solution.py:542
  122.7 0.0 copy-start.2
  122.7 1.3 copy-done.2
  124.0 17.0 %shard_map.54 = (bf16[64,8192]{1,0:T(8,128)(2,1)S(1)}, f32[32,32]{1,0:T(8,128)S(1)}, f32[8,128]{1,0:T(8,128)S(1)}, f32[128,32,128]{2,1,0:T(8,128)S(1)}) custom-call(s32[256]{0:T(256)S(1)} %fusion.cols, bf16[64,512,256]{2,1,0:T(8,128)(2,1)} %get-tuple-element.25.refs_0_, bf16[64,256,512]{2,1,0:T(8,128)(2,1)} %get-tuple-element.26.refs_1_, ...), custom_call_target="tpu_custom_call" | custom-call | tf_op jit(solution)/shard_map/pallas_call | solution.py:185
  141.0 43.2 %shard_map.55 = (f32[4,4,2,4,32,128]{5,4,3,2,1,0:T(8,128)S(1)}, f32[32,1024]{1,0:T(8,128)S(1)}, f32[3,32,32]{2,1,0:T(8,128)S(1)}, f32[32,1024]{1,0:T(8,128)}) custom-call(f32[4,4,2,4,32,128]{5,4,3,2,1,0:T(8,128)S(1)} %bitcast.8, f32[8,128]{1,0:T(8,128)S(1)} %get-tuple-element.38.refs_1_, f32[32,1024]{1,0:T(8,128)S(1)} %get-tuple-element.39.refs_2_.refs_8_, ...), custom_call_target="tpu_custom_call" | custom-call | tf_op jit(solution)/shard_map/pallas_call | solution.py:542
  184.2 0.0 copy-start.1
  184.2 12.6 %shard_map.56 = (bf16[64,8192]{1,0:T(8,128)(2,1)S(1)}, f32[32,32]{1,0:T(8,128)}, f32[8,128]{1,0:T(8,128)S(1)}) custom-call(s32[256]{0:T(256)S(1)} %fusion.cols, bf16[64,512,256]{2,1,0:T(8,128)(2,1)} %get-tuple-element.25.refs_0_, f32[128,32,128]{2,1,0:T(8,128)S(1)} %bitcast.6, bf16[64,8192]{1,0:T(8,128)(2,1)S(1)} %get-tuple-element.42.refs_2_.refs_5_, ...), custom_call_target="tpu_custom_call" | custom-call | tf_op jit(solution)/shard_map/pallas_call | solution.py:185
  196.8 0.0 copy-done.1
  196.8 19.2 %shard_map.57 = (f32[32,1024]{1,0:T(8,128)S(1)}, f32[32,8192]{1,0:T(8,128)S(1)}) custom-call(f32[8,128]{1,0:T(8,128)S(1)} %get-tuple-element.45.refs_0_, f32[3,32,32]{2,1,0:T(8,128)S(1)} %get-tuple-element.35.refs_4_.refs_3_.refs_5_.refs_1_, f32[3,32,32]{2,1,0:T(8,128)S(1)} %get-tuple-element.43.refs_4_.refs_2_, f32[32,8192]{1,0:T(8,128)S(1)} %copy-done.1, ...), custom_call_target="tpu_custom_call" | custom-call | tf_op jit(solution)/shard_map/pallas_call | solution.py:609
  216.0 0.7 copy.8
  216.6 1.0 copy.9
  (1 shorter events, 0.0 us)
Async XLA Ops:
  1.5 1.2 copy-start
  122.7 1.3 copy-start.2
  184.2 12.6 %copy-start.1 = (f32[32,8192]{1,0:T(8,128)S(1)}, f32[32,8192]{1,0:T(8,128)}, u32[]{:S(2)}) copy-start(f32[32,8192]{1,0:T(8,128)} %refs_3_.1) | copy-start | bytes 3145732

commit v3 on v0

v3 whole, which is shorter than its diff:
```python
import functools

import jax
import jax.numpy as jnp
from jax import lax
from jax.experimental import pallas as pl
from jax.experimental.pallas import tpu as pltpu
from jax.sharding import PartitionSpec as P

MESH = pl.DeviceIdType.MESH
F32 = jnp.float32
BF16 = jnp.bfloat16
ITERS = 3
CBD = 8
N = 32
B = 128
MIB = 2**20


def dot(a, b, ca, cb, precision=None):
    return lax.dot_general(
        a, b, (((ca,), (cb,)), ((), ())), precision=precision, preferred_element_type=F32
    )


def exact(a, b, ca=1, cb=0):
    return dot(a, b, ca, cb, lax.Precision.HIGHEST)


def split(x):
    hi = x.astype(BF16)
    lo = (x - hi.astype(F32)).astype(BF16)
    return hi, lo


def stacked(x):
    hi, lo = split(x)
    return jnp.concatenate([hi, lo], axis=0)


def pack(square):
    return jnp.concatenate([square[8 * g : 8 * g + 8] for g in range(4)], axis=1)


def unpack(tile):
    return jnp.concatenate([tile[:, N * g : N * g + N] for g in range(4)], axis=0)


def fold(square):
    half = square[:N] + square[N:]
    return half[:, :N] + half[:, N:]


def spd_solve(matrix, right):
    table = jnp.concatenate([matrix, right], axis=1)
    wide = (8, 2 * N)
    parts = [table[8 * g : 8 * g + 8] for g in range(4)]
    sub = lax.broadcasted_iota(jnp.int32, wide, 0)

    def lanes(group, b):
        return jnp.broadcast_to(group[:, b : b + 1], wide)

    def rows(group, a):
        return jnp.broadcast_to(group[a : a + 1], wide)

    for g in range(4):
        mine = parts[g]
        pivots = [lanes(mine, 8 * g + b) for b in range(8)]
        factors = [[lanes(parts[h], 8 * g + b) for b in range(8)] if h != g else None for h in range(4)]
        for a in range(8):
            inverse = 1.0 / rows(pivots[a], a)
            here = sub == a
            factor = pivots[a]
            for b in range(a + 1, 8):
                scaled = rows(pivots[b], a) * inverse
                pivots[b] = jnp.where(here, scaled, pivots[b] - factor * scaled)
            scaled = rows(mine, a) * inverse
            mine = jnp.where(here, scaled, mine - factor * scaled)
        parts[g] = mine
        for h in range(4):
            if h != g:
                for b in range(8):
                    parts[h] = parts[h] - factors[h][b] * rows(mine, b)
    return jnp.concatenate(parts, axis=0)[:, N : 2 * N]


def apply_t(square, both):
    hi, lo = split(square.T)
    left = jnp.concatenate([jnp.concatenate([hi, hi], axis=1), jnp.concatenate([lo, lo], axis=1)], axis=0)
    out = dot(left, both, 1, 0)
    return out[:N] + out[N:]


COL, ORDER, FIRST, LAST, SOME = range(5)


def order_kernel(cols, table):
    count = cols.shape[1]
    shape = (count, count)
    row = cols[...].astype(F32)
    across = jnp.broadcast_to(row, shape)
    down = across.T
    p = lax.broadcasted_iota(jnp.int32, shape, 0).astype(F32)
    q = lax.broadcasted_iota(jnp.int32, shape, 1).astype(F32)
    one = jnp.ones(shape, F32)
    zero = jnp.zeros(shape, F32)
    before = jnp.where((across < down) | ((across == down) & (q < p)), one, zero)
    twins = jnp.where((across == down) & (q < p), one, zero)
    rank = jnp.sum(before, axis=1, keepdims=True)
    alone = jnp.where(jnp.sum(twins, axis=1, keepdims=True) == 0.0, 1.0, 0.0)
    place = rank == q
    table[COL : COL + 1, :] = cols[...]
    table[ORDER : ORDER + 1, :] = jnp.sum(jnp.where(place, p, zero), axis=0, keepdims=True).astype(jnp.int32)
    table[FIRST : FIRST + 1, :] = jnp.sum(jnp.where(place, alone, zero), axis=0, keepdims=True).astype(jnp.int32)
    upto = jnp.sum(jnp.where(down <= q, one, zero), axis=0, keepdims=True)
    table[LAST : LAST + 1, :] = jnp.maximum(upto - 1.0, 0.0).astype(jnp.int32)
    some = jnp.sum(jnp.where(down == q, one, zero), axis=0, keepdims=True)
    table[SOME : SOME + 1, :] = jnp.where(some > 0.0, 1.0, 0.0).astype(jnp.int32)
    table[5:8, :] = jnp.zeros((3, count), jnp.int32)


def order_of(cols):
    return pl.pallas_call(
        order_kernel, out_shape=jax.ShapeDtypeStruct((8, cols.shape[1]), jnp.int32)
    )(cols)


class Traffic:
    def __init__(self, send_sem, recv_sem):
        self.send_sem, self.recv_sem = send_sem, recv_sem
        self.sent = []

    def send(self, slot, src, dst, device):
        copy = pltpu.make_async_remote_copy(
            src_ref=src,
            dst_ref=dst,
            send_sem=self.send_sem.at[slot],
            recv_sem=self.recv_sem.at[slot],
            device_id=device,
            device_id_type=MESH,
        )
        copy.start()
        self.sent.append(copy)
        return copy

    def finish(self):
        for copy in self.sent:
            copy.wait_send()
        self.sent = []


class Plane:
    def __init__(self, row, col):
        z, x = row // 4, lax.rem(row, 4)

        def along_x(d):
            return (z * 4 + lax.rem(x + d, 4), col)

        def along_z(d):
            return (lax.rem(z + d, 4) * 4 + x, col)

        self.z, self.x = z, x
        self.halves = ((x, z, along_x, along_z), (z, x, along_z, along_x))


def chunk(ref, h, ta, tb, s):
    zz, xx = (tb, ta) if h == 0 else (ta, tb)
    return ref.at[zz, xx, h] if s is None else ref.at[zz, xx, h, pl.ds(2 * s, 2)]


RS_SLOTS = 60
AG_SLOTS = 40
SUM_SLOTS = 10
OFFSETS = (2, 3, 1, 0)


def reduce_scatter(sums, plane, r1, p1, r2, tr, hook):
    c1, c2 = {}, {}
    halves = plane.halves

    def send1(u, h, idx):
        pa, pb, ring, _ = halves[h]
        tb = lax.rem(pb + OFFSETS[u], 4)
        off, s, d = ((2, 0, 1), (2, 1, 3), (1, 1, 1), (3, 0, 3))[idx]
        src = chunk(sums, h, lax.rem(pa + off, 4), tb, s)
        c1[u, h, idx] = tr.send((h * 4 + u) * 6 + idx, src, r1.at[h, u, idx], ring(d))

    def pass_on(u, h):
        pa, pb, ring, _ = halves[h]
        tb = lax.rem(pb + OFFSETS[u], 4)
        for idx, off, d in ((0, 1, 1), (1, 3, 3)):
            c1[u, h, idx].wait_recv()
            r1[h, u, idx] += chunk(sums, h, lax.rem(pa + off, 4), tb, idx)[...]
            c1[u, h, 4 + idx] = tr.send(
                (h * 4 + u) * 6 + 4 + idx, r1.at[h, u, idx], r1.at[h, u, 4 + idx], ring(d)
            )

    def send2(h, idx, src, d):
        c2[h, idx] = tr.send(48 + h * 6 + idx, src, r2.at[h, idx], halves[h][3](d))

    def close(u, h):
        pa, pb, _, _ = halves[h]
        tb = lax.rem(pb + OFFSETS[u], 4)
        for idx in (2, 3, 4, 5):
            c1[u, h, idx].wait_recv()
        p1[h, u, 0:2] = chunk(sums, h, pa, tb, 0)[...] + (r1[h, u, 3] + r1[h, u, 4])
        p1[h, u, 2:4] = chunk(sums, h, pa, tb, 1)[...] + (r1[h, u, 2] + r1[h, u, 5])
        if u == 0:
            send2(h, 0, p1.at[h, 0, pl.ds(0, 2)], 1)
            send2(h, 1, p1.at[h, 0, pl.ds(2, 2)], 3)
        if u == 1:
            send2(h, 3, p1.at[h, 1, pl.ds(0, 2)], 3)
            c2[h, 1].wait_recv()
            r2[h, 1] += p1[h, 1, 2:4]
            send2(h, 5, r2.at[h, 1], 3)
        if u == 2:
            send2(h, 2, p1.at[h, 2, pl.ds(2, 2)], 1)
            c2[h, 0].wait_recv()
            r2[h, 0] += p1[h, 2, 0:2]
            send2(h, 4, r2.at[h, 0], 1)

    both = range(2)
    for u in range(4):
        for h in both:
            send1(u, h, 0)
            send1(u, h, 1)
    for h in both:
        send1(0, h, 2)
        send1(0, h, 3)
    hook(-1)
    for u in range(5):
        if u < 4:
            for h in both:
                pass_on(u, h)
            if u < 3:
                for h in both:
                    send1(u + 1, h, 2)
                    send1(u + 1, h, 3)
        if u >= 1:
            for h in both:
                close(u - 1, h)
        hook(u)
    own = []
    for h in both:
        for idx in (2, 3, 4, 5):
            c2[h, idx].wait_recv()
        first = p1[h, 3, 0:2] + (r2[h, 3] + r2[h, 4])
        second = p1[h, 3, 2:4] + (r2[h, 2] + r2[h, 5])
        own += [first[0], first[1], second[0], second[1]]
    tr.finish()
    return jnp.concatenate(own, axis=1)


HOPS = ((0, None, 1), (0, None, 3), (3, 0, 1), (1, 1, 3))


def gather_all(vec, plane, tr, hook):
    halves = plane.halves
    order = (0, 3, 1, 2)
    c1, c2 = {}, {}

    def send1(h, idx):
        pa, pb, _, ring = halves[h]
        off, s, d = HOPS[idx]
        ref = chunk(vec, h, pa, lax.rem(pb + off, 4), s)
        c1[h, idx] = tr.send(RS_SLOTS + h * 4 + idx, ref, ref, ring(d))

    def send2(h, v, idx):
        pa, pb, ring, _ = halves[h]
        tb = lax.rem(pb + order[v], 4)
        off, s, d = HOPS[idx]
        ref = chunk(vec, h, lax.rem(pa + off, 4), tb, s)
        c2[h, v, idx] = tr.send(RS_SLOTS + 8 + (h * 4 + v) * 4 + idx, ref, ref, ring(d))

    both = range(2)

    def unit(v):
        for h in both:
            send2(h, v, 0)
            send2(h, v, 1)

    def pass_on(v):
        for h in both:
            for idx in range(2):
                c2[h, v, idx].wait_recv()
                send2(h, v, 2 + idx)

    for h in both:
        send1(h, 0)
        send1(h, 1)
    unit(0)
    hook(0)
    for h in both:
        for idx in range(2):
            c1[h, idx].wait_recv()
            send1(h, 2 + idx)
    unit(1)
    pass_on(0)
    unit(2)
    hook(1)
    for h in both:
        c1[h, 2].wait_recv()
        c1[h, 3].wait_recv()
    unit(3)
    pass_on(1)
    hook(2)
    pass_on(2)
    hook(3)
    pass_on(3)
    hook(4)
    for v in range(4):
        for h in both:
            c2[h, v, 2].wait_recv()
            c2[h, v, 3].wait_recv()
    tr.finish()


def sum_stages(row, col, n_col):
    n_y = n_col // 2
    z, x = row // 4, lax.rem(row, 4)
    y, core = col // 2, lax.rem(col, 2)
    return [
        ([(row, y * 2 + 1 - core)], core, 2),
        ([(row, lax.rem(y + d, n_y) * 2 + core) for d in range(1, n_y)], y, n_y),
        ([(z * 4 + lax.rem(x + d, 4), col) for d in range(1, 4)], x, 4),
        ([(lax.rem(z + d, 4) * 4 + x, col) for d in range(1, 4)], z, 4),
    ]


class TileSum:
    def __init__(self, stages, tr, slot, box, rows):
        self.stages, self.tr, self.slot, self.box, self.rows = stages, tr, slot, box, rows
        self.at, self.open = 0, []

    def put(self, tile):
        peers, me, _ = self.stages[self.at]
        ref = self.box.at[self.at, me, pl.ds(0, self.rows)]
        self.box[self.at, me, 0 : self.rows] = tile
        self.open = []
        for device in peers:
            self.open.append(self.tr.send(self.slot, ref, ref, device))
            self.slot += 1

    def take(self):
        for c in self.open:
            c.wait_recv()
        total = self.box[self.at, 0, 0 : self.rows]
        for i in range(1, self.stages[self.at][2]):
            total = total + self.box[self.at, i, 0 : self.rows]
        self.at += 1
        return total

    def step(self):
        self.put(self.take())


GG, IG, MIX, STEP = range(4)
ROWS = 64
UNROLL = 8
LOAD = 4
SLOTS = 4


def rows_loop(lo, hi, width, step):
    def some(o, carry):
        for j in range(width):
            step(lo + o * width + j)
        return carry

    lax.fori_loop(0, (hi - lo) // width, some, 0)


def cgls_kernel(n_col, table, blocks, targets, sol, res, *scratch):
    across, down, pieces, running, sums, vec, parts, images, t_mem, grads = scratch[:10]
    conj, gram_acc, small, r1, p1, r2, box, send_sem, recv_sem, load_sem = scratch[10:]
    row, col = lax.axis_index("row"), lax.axis_index("col")
    plane = Plane(row, col)
    stages = sum_stages(row, col, n_col)
    tr, tr_small = Traffic(send_sem, recv_sem), Traffic(send_sem, recv_sem)

    size = LOAD * 16

    def load(step):
        slot = lax.rem(step, SLOTS)
        return pltpu.make_async_copy(
            blocks.at[pl.ds(step * size, size)], running.at[pl.ds(slot * size, size)], load_sem.at[slot]
        )

    read_targets = pltpu.make_async_copy(targets, t_mem, load_sem.at[SLOTS])
    read_targets.start()
    for s in range(SLOTS):
        load(s).start()

    barrier = pltpu.get_barrier_semaphore()
    who = [device for peers, _, _ in stages for device in peers]
    for device in who:
        pl.semaphore_signal(barrier, inc=1, device_id=device, device_id_type=MESH)

    def lanes(i):
        return pl.ds(pl.multiple_of(i * B, B), B)

    def piece(i, both, block):
        out = dot(jnp.concatenate([both, both], axis=1), block, 1, 0)
        out = out[:N] + out[N:]
        for k in range(4):
            pieces[i * 4 + k] = out[:, k * B : (k + 1) * B]

    read_targets.wait()

    def first(step, carry):
        load(step).wait()
        slot = lax.rem(step, SLOTS)
        for j in range(LOAD):
            i = step * LOAD + j
            his, los = [], []
            for k in range(4):
                base = slot * size + j * 16 + k * 4
                hi, lo = split(jnp.concatenate([running[base + q] for q in range(4)], axis=0))
                his.append(hi)
                los.append(lo)
            block = jnp.concatenate([jnp.concatenate(his, axis=1), jnp.concatenate(los, axis=1)], axis=0)
            across[i] = block
            piece(i, stacked(t_mem[:, lanes(i)]), block)

        @pl.when(step + SLOTS < ROWS // LOAD)
        def _():
            load(step + SLOTS).start()

        return carry

    lax.fori_loop(0, ROWS // LOAD, first, 0)

    def add_up():
        def run(o, total):
            for j in range(8):
                p = o * 8 + j
                total = jnp.where(table[FIRST, p] == 1, 0.0, total) + pieces[table[ORDER, p]]
                running[p] = total
            return total

        lax.fori_loop(0, ROWS * 4 // 8, run, jnp.zeros((N, B), F32))

        def pick(owner, carry):
            for h in range(2):
                for j in range(4):
                    c = owner * CBD + 4 * h + j
                    value = jnp.where(table[SOME, c] == 1, running[table[LAST, c]], 0.0)
                    sums[owner // 4, lax.rem(owner, 4), h, j] = value
            return carry

        lax.fori_loop(0, 16, pick, 0)

    def turn(i):
        for k in range(4):
            for h in range(2):
                tile = across[i, h * B : (h + 1) * B, k * B : (k + 1) * B]
                down[i, k * B : (k + 1) * B, h * B : (h + 1) * B] = tile.T

    def forward(at):
        def one(i):
            picked = jnp.concatenate([parts[table[COL, i * 4 + j]] for j in range(4)], axis=1)
            quad = dot(picked, down[i], 1, 0)
            quad = quad[:N] + quad[N:]
            images[at : at + 2 * N, lanes(i)] = stacked(quad[:, :B] + quad[:, B:])

        return one

    def backward(at):
        def one(i):
            piece(i, images[at : at + 2 * N, lanes(i)], across[i])

        return one

    def image_grams(k):
        gram_acc[...] = jnp.zeros_like(gram_acc)
        width = 1024

        def strip(s, carry):
            at = pl.ds(pl.multiple_of(s * width, width), width)
            mine = images[2 * N * k : 2 * N * (k + 1), at]
            gram_acc[:, 0 : 2 * N * (k + 1)] += dot(mine, images[0 : 2 * N * (k + 1), at], 1, 1)
            return carry

        lax.fori_loop(0, ROWS * B // width, strip, 0)
        return jnp.concatenate(
            [pack(fold(gram_acc[:, 2 * N * j : 2 * N * (j + 1)])) for j in range(k, -1, -1)], axis=0
        )

    def mix_of(k):
        if k:
            small[k, MIX] = spd_solve(small[k - 1, GG], small[k, GG])

    def image_gram_of(k, total):
        gram = unpack(total[0:8])
        if k:
            mix = small[k, MIX]
            cross = unpack(total[8:16])
            if k == 2:
                cross = cross + exact(unpack(total[16:24]), small[1, MIX])
            mixed = exact(cross, mix)
            gram = gram + (mixed + mixed.T) + exact(mix, exact(small[k - 1, IG], mix), 0, 0)
        small[k, IG] = gram

    def cut(owner, carry):
        for h in range(2):
            for j in range(4):
                parts[owner * CBD + 4 * h + j] = stacked(vec[owner // 4, lax.rem(owner, 4), h, j])
        return carry

    add_up()
    pl.semaphore_wait(barrier, len(who))
    slot0 = RS_SLOTS + AG_SLOTS
    turned = {-1: (0, 12), 0: (12, 16), 1: (16, 20), 2: (20, 24), 3: (24, 28), 4: (28, 32)}
    turned_later = {0: (32, 42), 1: (42, 50), 2: (50, 56), 3: (56, 60), 4: (60, 64)}
    image_total = None
    for k in range(ITERS):

        def beside_first(u, k=k):
            if k == 0:
                rows_loop(*turned[u], 2, turn)
            elif u == -1:
                mix_of(k - 1)
            elif u == 0:
                image_gram_of(k - 1, image_total)
            elif u == 1:
                small[k - 1, STEP] = spd_solve(small[k - 1, IG], small[k - 1, GG])

        fresh = reduce_scatter(sums, plane, r1, p1, r2, tr, beside_first)
        if k == 0:
            grad = fresh
        else:
            direction = fresh if k == 1 else fresh + apply_t(small[1, MIX], stacked(conj[...]))
            grad = grads[k - 1] - apply_t(small[k - 1, STEP], stacked(direction))
        for h in range(2):
            for j in range(4):
                at = (4 * h + j) * B
                vec[plane.z, plane.x, h, j] = grad[:, at : at + B]
        grad_sum = TileSum(stages, tr_small, slot0 + 2 * k * SUM_SLOTS, box.at[2 * k], 8)

        def beside_second(v, k=k):
            if v == 0:
                both = stacked(grad)
                grad_sum.put(pack(fold(dot(both, both, 1, 1))))
                grads[k] = grad
                if k:
                    conj[...] = direction
            if v == 2:
                grad_sum.step()
            if k == 0:
                rows_loop(*turned_later[v], 2, turn)

        gather_all(vec, plane, tr, beside_second)
        grad_sum.step()
        lax.fori_loop(0, 16, cut, 0)
        rows_loop(0, ROWS // 2, UNROLL, forward(2 * N * k))
        grad_sum.step()
        rows_loop(ROWS // 2, ROWS, UNROLL, forward(2 * N * k))
        small[k, GG] = unpack(grad_sum.take())
        image_sum = TileSum(stages, tr_small, slot0 + (2 * k + 1) * SUM_SLOTS, box.at[2 * k + 1], 8 * (k + 1))
        image_sum.put(image_grams(k))
        if k + 1 < ITERS:
            rows_loop(0, 24, UNROLL, backward(2 * N * k))
            image_sum.step()
            rows_loop(24, 40, UNROLL, backward(2 * N * k))
            image_sum.step()
            rows_loop(40, ROWS, UNROLL, backward(2 * N * k))
            image_sum.step()
            add_up()
            image_total = image_sum.take()
        else:
            mix_of(k)
            for _ in range(3):
                image_sum.step()
            image_gram_of(k, image_sum.take())

    e2 = spd_solve(small[2, IG], small[2, GG])
    e1 = small[1, STEP] + exact(small[2, MIX], e2)
    e0 = small[0, STEP] + exact(small[1, MIX], e1)
    his, los = [], []
    for e in (e0, e1, e2):
        hi, lo = split(e.T)
        his += [hi, hi]
        los += [lo, lo]
    left = jnp.concatenate([jnp.concatenate(his, axis=1), jnp.concatenate(los, axis=1)], axis=0)
    out = dot(left, jnp.concatenate([stacked(grads[j]) for j in range(3)], axis=0), 1, 0)
    sol[...] = out[:N] + out[N:]
    width = 1024

    def strip(s, carry):
        at = pl.ds(pl.multiple_of(s * width, width), width)
        out = dot(left, images[:, at], 1, 0)
        res[:, at] = t_mem[:, at] - (out[:N] + out[N:])
        return carry

    lax.fori_loop(0, ROWS * B // width, strip, 0)
    tr_small.finish()


def body(blocks, block_cols, targets):
    n_row = lax.axis_size("row")
    n_col = lax.axis_size("col")
    group = CBD * n_row
    flat = block_cols.reshape(1, -1)
    table = order_of(flat // (CBD * n_col) * CBD + lax.rem(flat, CBD))
    vmem = pl.BlockSpec(memory_space=pltpu.VMEM)
    anywhere = pl.BlockSpec(memory_space=pl.ANY)
    width = CBD * B
    chunks = (4, 4, 2, CBD // 2, N, B)
    slots = RS_SLOTS + AG_SLOTS + 6 * SUM_SLOTS
    return tuple(
        pl.pallas_call(
            functools.partial(cgls_kernel, n_col),
            out_shape=[jax.ShapeDtypeStruct((N, width), F32), jax.ShapeDtypeStruct(targets.shape, F32)],
            in_specs=[pl.BlockSpec(memory_space=pltpu.SMEM), anywhere, anywhere],
            out_specs=[vmem] * 2,
            scratch_shapes=[
                pltpu.VMEM((ROWS, 2 * B, 4 * B), BF16),
                pltpu.VMEM((ROWS, 4 * B, 2 * B), BF16),
                pltpu.VMEM((ROWS * 4, N, B), F32),
                pltpu.VMEM((ROWS * 4, N, B), F32),
                pltpu.VMEM(chunks, F32),
                pltpu.VMEM(chunks, F32),
                pltpu.VMEM((group, 2 * N, B), BF16),
                pltpu.VMEM((2 * N * ITERS, ROWS * B), BF16),
                pltpu.VMEM((N, ROWS * B), F32),
                pltpu.VMEM((ITERS, N, width), F32),
                pltpu.VMEM((N, width), F32),
                pltpu.VMEM((2 * N, 2 * N * 4), F32),
                pltpu.VMEM((ITERS, 4, N, N), F32),
                pltpu.VMEM((2, 4, 6, 2, N, B), F32),
                pltpu.VMEM((2, 4, 4, N, B), F32),
                pltpu.VMEM((2, 6, 2, N, B), F32),
                pltpu.VMEM((6, 4, 4, 24, B), F32),
                pltpu.SemaphoreType.DMA((slots,)),
                pltpu.SemaphoreType.DMA((slots,)),
                pltpu.SemaphoreType.DMA((SLOTS + 1,)),
            ],
            compiler_params=pltpu.CompilerParams(
                collective_id=0, has_side_effects=True, vmem_limit_bytes=60 * MIB
            ),
        )(table, blocks.reshape(-1, N, B), targets)
    )


def solution(mesh):
    placed = (P(("row", "col"), None, None, None), P(("row", "col"), None), P(None, ("row", "col")))
    return jax.shard_map(
        body,
        mesh=mesh,
        in_specs=placed,
        out_specs=(P(None, ("row", "col")), P(None, ("row", "col"))),
        check_vma=False,
    )
```

time: 837 us -> 189 us (0.23)
  blocking collectives: 264 us -> 0 us
  waiting for transfers between devices: 245 us -> 0 us
  Pallas kernels: 0 us -> 182 us
  matrix products: 137 us -> 0 us
  other arithmetic: 134 us -> 0.58 us
  local copies, waits for them, and re-layouts: 33.8 us -> 4.71 us
  between operations: 14.7 us -> 0.64 us
    psum x6 -> x0, blocking collectives: 264 us -> none  [the longest x3 197 us: body(): image_gram = lax.psum(gram_of(image), ('row', 'col'))]
    psum x3 -> x0, waiting for transfers between devices: 245 us -> none  [gradient_of(): gradient = lax.psum(backward(resid), 'row')]
    pallas_call x0 -> x2, Pallas kernels: none -> 182 us  [the longest x1 180 us: body(): pl.pallas_call(functools.partial(cgls_kernel, n_col), out_shape=[jax.Shap...]
    dot_general x20 -> x0, matrix products: 135 us -> none  [the longest x3 58.2 us: body(): jnp.einsum('ikab,nikb->nia', blocks, picked, precision=lax.Precision.HIGH...]
    scatter-add x3 -> x0, other arithmetic: 90.6 us -> none  [backward(): jax.ops.segment_sum(pieces_all, local_cols, num_segments=group_size)]
    another operation x25 -> x0, other arithmetic: 33.4 us -> none  [the longest x15 18 us: chol_solve(): lower_factor = jnp.linalg.cholesky(matrix)]
    reshape x8 -> x1, local copies, waits for them, and re-layouts: 11.6 us -> 0.1 us  [body(): flat = block_cols.reshape(1, -1)]
    gather x3 -> x0, local copies, waits for them, and re-layouts: 10.3 us -> none  [body(): jnp.take(tiles, local_cols, axis=1)]
  transfers between devices with their start and end apart: 3 -> 0, of which waited for: 3 -> 0; matrix products, arithmetic and copies ran while one was open for 3% -> 0% of each run, Pallas kernels for 0% -> 0%
where the time goes in v3:
time: 189 us; the launch traced here: 187 us
  Pallas kernels  182 us (96%)
  local copies, waits for them, and re-layouts  4.71 us (2%)
    pallas_call x1, Pallas kernels, body(): pl.pallas_call(functools.partial(cgls_kernel, n_col), out_shape=[jax.Shap...  180 us
    unnamed x3, local copies, waits for them, and re-layouts  4.6 us

profile of v3, /device:TPU:1, one launch (start us, length us, event | category | flops | bytes accessed | tf_op | source)
XLA Modules:
  0.0 187.5 jit_solution(14611449621283688745)
XLA Ops:
  0.6 0.8 copy.6
  1.4 0.1 reshape.140
  1.5 0.6 fusion.cols
  2.1 1.5 shard_map.50.table
  3.6 180.0 %shard_map.51 = (f32[32,1024]{1,0:T(8,128)}, f32[32,8192]{1,0:T(8,128)}) custom-call(s32[8,256]{1,0:T(8,128)} %shard_map.50.table, f32[1024,32,128]{2,1,0:T(8,128)} %bitcast.1, f32[32,8192]{1,0:T(8,128)} %targets.1), custom_call_target="tpu_custom_call" | custom-call | tf_op jit(solution)/shard_map/pallas_call | solution.py:611
  183.6 1.6 copy.9
  185.2 2.3 %copy.10 = f32[32,8192]{1,0:T(8,128)} copy(f32[32,8192]{1,0:T(8,128)} %get-tuple-element.5) | data formatting | bytes 2097152

commit v4 on v3

--- a/solution.py
+++ b/solution.py
@@ -170,7 +170,7 @@
 
 RS_SLOTS = 60
 AG_SLOTS = 40
-SUM_SLOTS = 10
+SUM_SLOTS = 22
 OFFSETS = (2, 3, 1, 0)
 
 
@@ -315,16 +315,13 @@
     tr.finish()
 
 
-def sum_stages(row, col, n_col):
-    n_y = n_col // 2
+def sum_stages(row, col, n_row, n_col):
     z, x = row // 4, lax.rem(row, 4)
-    y, core = col // 2, lax.rem(col, 2)
-    return [
-        ([(row, y * 2 + 1 - core)], core, 2),
-        ([(row, lax.rem(y + d, n_y) * 2 + core) for d in range(1, n_y)], y, n_y),
-        ([(z * 4 + lax.rem(x + d, 4), col) for d in range(1, 4)], x, 4),
-        ([(lax.rem(z + d, 4) * 4 + x, col) for d in range(1, 4)], z, 4),
-    ]
+    along_x = ([(z * 4 + lax.rem(x + d, 4), col) for d in range(1, 4)], x, 4)
+    along_z = ([(lax.rem(z + d, 4) * 4 + x, col) for d in range(1, 4)], z, 4)
+    plane = ([(lax.rem(row + d, n_row), col) for d in range(1, n_row)], row, n_row)
+    across = ([(row, lax.rem(col + d, n_col)) for d in range(1, n_col)], col, n_col)
+    return along_x, along_z, plane, across
 
 
 class TileSum:
@@ -370,12 +367,12 @@
     lax.fori_loop(0, (hi - lo) // width, some, 0)
 
 
-def cgls_kernel(n_col, table, blocks, targets, sol, res, *scratch):
+def cgls_kernel(n_row, n_col, table, blocks, targets, sol, res, *scratch):
     across, down, pieces, running, sums, vec, parts, images, t_mem, grads = scratch[:10]
     conj, gram_acc, small, r1, p1, r2, box, send_sem, recv_sem, load_sem = scratch[10:]
     row, col = lax.axis_index("row"), lax.axis_index("col")
     plane = Plane(row, col)
-    stages = sum_stages(row, col, n_col)
+    along_x, along_z, in_plane, across_it = sum_stages(row, col, n_row, n_col)
     tr, tr_small = Traffic(send_sem, recv_sem), Traffic(send_sem, recv_sem)
 
     size = LOAD * 16
@@ -392,7 +389,7 @@
         load(s).start()
 
     barrier = pltpu.get_barrier_semaphore()
-    who = [device for peers, _, _ in stages for device in peers]
+    who = in_plane[0] + across_it[0]
     for device in who:
         pl.semaphore_signal(barrier, inc=1, device_id=device, device_id_type=MESH)
 
@@ -512,7 +509,7 @@
     slot0 = RS_SLOTS + AG_SLOTS
     turned = {-1: (0, 12), 0: (12, 16), 1: (16, 20), 2: (20, 24), 3: (24, 28), 4: (28, 32)}
     turned_later = {0: (32, 42), 1: (42, 50), 2: (50, 56), 3: (56, 60), 4: (60, 64)}
-    image_total = None
+    image_sum = None
     for k in range(ITERS):
 
         def beside_first(u, k=k):
@@ -521,7 +518,7 @@
             elif u == -1:
                 mix_of(k - 1)
             elif u == 0:
-                image_gram_of(k - 1, image_total)
+                image_gram_of(k - 1, image_sum.take())
             elif u == 1:
                 small[k - 1, STEP] = spd_solve(small[k - 1, IG], small[k - 1, GG])
 
@@ -535,7 +532,7 @@
             for j in range(4):
                 at = (4 * h + j) * B
                 vec[plane.z, plane.x, h, j] = grad[:, at : at + B]
-        grad_sum = TileSum(stages, tr_small, slot0 + 2 * k * SUM_SLOTS, box.at[2 * k], 8)
+        grad_sum = TileSum([across_it, along_x, along_z], tr_small, slot0 + 2 * k * SUM_SLOTS, box.at[2 * k], 8)
 
         def beside_second(v, k=k):
             if v == 0:
@@ -544,33 +541,35 @@
                 grads[k] = grad
                 if k:
                     conj[...] = direction
-            if v == 2:
-                grad_sum.step()
             if k == 0:
                 rows_loop(*turned_later[v], 2, turn)
 
         gather_all(vec, plane, tr, beside_second)
         grad_sum.step()
         lax.fori_loop(0, 16, cut, 0)
-        rows_loop(0, ROWS // 2, UNROLL, forward(2 * N * k))
+        rows_loop(0, 40, UNROLL, forward(2 * N * k))
         grad_sum.step()
-        rows_loop(ROWS // 2, ROWS, UNROLL, forward(2 * N * k))
-        small[k, GG] = unpack(grad_sum.take())
-        image_sum = TileSum(stages, tr_small, slot0 + (2 * k + 1) * SUM_SLOTS, box.at[2 * k + 1], 8 * (k + 1))
+        rows_loop(40, ROWS, UNROLL, forward(2 * N * k))
+        last = k + 1 == ITERS
+        image_sum = TileSum(
+            [in_plane, across_it] if last else [along_x, along_z, across_it],
+            tr_small,
+            slot0 + (2 * k + 1) * SUM_SLOTS,
+            box.at[2 * k + 1],
+            8 * (k + 1),
+        )
         image_sum.put(image_grams(k))
-        if k + 1 < ITERS:
-            rows_loop(0, 24, UNROLL, backward(2 * N * k))
-            image_sum.step()
-            rows_loop(24, 40, UNROLL, backward(2 * N * k))
+        if not last:
+            rows_loop(0, 40, UNROLL, backward(2 * N * k))
+            small[k, GG] = unpack(grad_sum.take())
             image_sum.step()
             rows_loop(40, ROWS, UNROLL, backward(2 * N * k))
+            add_up()
             image_sum.step()
-            add_up()
-            image_total = image_sum.take()
         else:
+            small[k, GG] = unpack(grad_sum.take())
             mix_of(k)
-            for _ in range(3):
-                image_sum.step()
+            image_sum.step()
             image_gram_of(k, image_sum.take())
 
     e2 = spd_solve(small[2, IG], small[2, GG])
@@ -609,7 +608,7 @@
     slots = RS_SLOTS + AG_SLOTS + 6 * SUM_SLOTS
     return tuple(
         pl.pallas_call(
-            functools.partial(cgls_kernel, n_col),
+            functools.partial(cgls_kernel, n_row, n_col),
             out_shape=[jax.ShapeDtypeStruct((N, width), F32), jax.ShapeDtypeStruct(targets.shape, F32)],
             in_specs=[pl.BlockSpec(memory_space=pltpu.SMEM), anywhere, anywhere],
             out_specs=[vmem] * 2,
@@ -630,7 +629,7 @@
                 pltpu.VMEM((2, 4, 6, 2, N, B), F32),
                 pltpu.VMEM((2, 4, 4, N, B), F32),
                 pltpu.VMEM((2, 6, 2, N, B), F32),
-                pltpu.VMEM((6, 4, 4, 24, B), F32),
+                pltpu.VMEM((6, 3, n_row, 24, B), F32),
                 pltpu.SemaphoreType.DMA((slots,)),
                 pltpu.SemaphoreType.DMA((slots,)),
                 pltpu.SemaphoreType.DMA((SLOTS + 1,)),

time: 189 us -> 174 us (0.921)
  Pallas kernels: 182 us -> 168 us
    pallas_call x1, Pallas kernels: 180 us -> 166 us  [body(): pl.pallas_call(functools.partial(cgls_kernel, n_row, n_col), out_shape=[j...]
where the time goes in v4:
time: 174 us
  Pallas kernels  168 us (97%)
  local copies, waits for them, and re-layouts  4.71 us (3%)
    pallas_call x1, Pallas kernels, body(): pl.pallas_call(functools.partial(cgls_kernel, n_row, n_col), out_shape=[j...  166 us
    unnamed x3, local copies, waits for them, and re-layouts  4.6 us

profile of v4, /device:TPU:1, one launch (start us, length us, event | category | flops | bytes accessed | tf_op | source)
XLA Modules:
  0.0 173.6 jit_solution(10442914352986983669)
XLA Ops:
  0.6 0.8 copy.6
  1.4 0.1 reshape.140
  1.5 0.6 fusion.cols
  2.1 1.5 shard_map.50.table
  3.6 166.2 %shard_map.51 = (f32[32,1024]{1,0:T(8,128)}, f32[32,8192]{1,0:T(8,128)}) custom-call(s32[8,256]{1,0:T(8,128)} %shard_map.50.table, f32[1024,32,128]{2,1,0:T(8,128)} %bitcast.1, f32[32,8192]{1,0:T(8,128)} %targets.1), custom_call_target="tpu_custom_call" | custom-call | tf_op jit(solution)/shard_map/pallas_call | solution.py:610
  169.8 1.6 copy.9
  171.4 2.3 %copy.10 = f32[32,8192]{1,0:T(8,128)} copy(f32[32,8192]{1,0:T(8,128)} %get-tuple-element.5) | data formatting | bytes 2097152

commit v5 on v4

--- a/solution.py
+++ b/solution.py
@@ -224,22 +224,34 @@
         for h in both:
             send1(u, h, 0)
             send1(u, h, 1)
-    for h in both:
-        send1(0, h, 2)
-        send1(0, h, 3)
-    hook(-1)
-    for u in range(5):
-        if u < 4:
-            for h in both:
-                pass_on(u, h)
-            if u < 3:
-                for h in both:
-                    send1(u + 1, h, 2)
-                    send1(u + 1, h, 3)
-        if u >= 1:
-            for h in both:
-                close(u - 1, h)
-        hook(u)
+    def plain(u):
+        for h in both:
+            send1(u, h, 2)
+            send1(u, h, 3)
+
+    def on(u):
+        for h in both:
+            pass_on(u, h)
+
+    def done(u):
+        for h in both:
+            close(u, h)
+
+    plain(0)
+    plain(1)
+    hook(0)
+    on(0)
+    on(1)
+    plain(2)
+    plain(3)
+    hook(1)
+    on(2)
+    done(0)
+    on(3)
+    done(1)
+    done(2)
+    done(3)
+    hook(2)
     own = []
     for h in both:
         for idx in (2, 3, 4, 5):
@@ -354,6 +366,7 @@
 GG, IG, MIX, STEP = range(4)
 ROWS = 64
 UNROLL = 8
+LEAD = UNROLL * B
 LOAD = 4
 SLOTS = 4
 
@@ -395,6 +408,11 @@
 
     def lanes(i):
         return pl.ds(pl.multiple_of(i * B, B), B)
+
+    def spot(i):
+        return pl.ds(pl.multiple_of(LEAD + i * B, B), B)
+
+    images[:, 0:LEAD] = jnp.zeros((2 * N * ITERS, LEAD), BF16)
 
     def piece(i, both, block):
         out = dot(jnp.concatenate([both, both], axis=1), block, 1, 0)
@@ -458,27 +476,34 @@
             picked = jnp.concatenate([parts[table[COL, i * 4 + j]] for j in range(4)], axis=1)
             quad = dot(picked, down[i], 1, 0)
             quad = quad[:N] + quad[N:]
-            images[at : at + 2 * N, lanes(i)] = stacked(quad[:, :B] + quad[:, B:])
+            images[at : at + 2 * N, spot(i)] = stacked(quad[:, :B] + quad[:, B:])
 
         return one
 
     def backward(at):
         def one(i):
-            piece(i, images[at : at + 2 * N, lanes(i)], across[i])
+            piece(i, images[at : at + 2 * N, spot(i)], across[i])
 
         return one
 
+    def add_gram(k, group):
+        at = pl.ds(pl.multiple_of(group * LEAD, LEAD), LEAD)
+        mine = images[2 * N * k : 2 * N * (k + 1), at]
+        gram_acc[:, 0 : 2 * N * (k + 1)] += dot(mine, images[0 : 2 * N * (k + 1), at], 1, 1)
+
+    def forward_groups(k, lo, hi):
+        row_of = forward(2 * N * k)
+
+        def group(g, carry):
+            add_gram(k, g)
+            for j in range(UNROLL):
+                row_of(g * UNROLL + j)
+            return carry
+
+        lax.fori_loop(lo, hi, group, 0)
+
     def image_grams(k):
-        gram_acc[...] = jnp.zeros_like(gram_acc)
-        width = 1024
-
-        def strip(s, carry):
-            at = pl.ds(pl.multiple_of(s * width, width), width)
-            mine = images[2 * N * k : 2 * N * (k + 1), at]
-            gram_acc[:, 0 : 2 * N * (k + 1)] += dot(mine, images[0 : 2 * N * (k + 1), at], 1, 1)
-            return carry
-
-        lax.fori_loop(0, ROWS * B // width, strip, 0)
+        add_gram(k, ROWS // UNROLL)
         return jnp.concatenate(
             [pack(fold(gram_acc[:, 2 * N * j : 2 * N * (j + 1)])) for j in range(k, -1, -1)], axis=0
         )
@@ -498,28 +523,33 @@
             gram = gram + (mixed + mixed.T) + exact(mix, exact(small[k - 1, IG], mix), 0, 0)
         small[k, IG] = gram
 
-    def cut(owner, carry):
+    def cut(h, ta, tb):
+        zz, xx = (tb, ta) if h == 0 else (ta, tb)
+        for j in range(4):
+            parts[(zz * 4 + xx) * CBD + 4 * h + j] = stacked(vec[zz, xx, h, j])
+
+    def cut_unit(v, offsets):
         for h in range(2):
-            for j in range(4):
-                parts[owner * CBD + 4 * h + j] = stacked(vec[owner // 4, lax.rem(owner, 4), h, j])
-        return carry
+            pa, pb, _, _ = plane.halves[h]
+            for off in offsets:
+                cut(h, lax.rem(pa + off, 4), lax.rem(pb + (0, 3, 1, 2)[v], 4))
 
     add_up()
     pl.semaphore_wait(barrier, len(who))
     slot0 = RS_SLOTS + AG_SLOTS
-    turned = {-1: (0, 12), 0: (12, 16), 1: (16, 20), 2: (20, 24), 3: (24, 28), 4: (28, 32)}
-    turned_later = {0: (32, 42), 1: (42, 50), 2: (50, 56), 3: (56, 60), 4: (60, 64)}
+    turned = {0: (0, 10), 1: (10, 22), 2: (22, 32)}
+    turned_later = {0: (32, 36), 1: (36, 46), 2: (46, 52), 3: (52, 56), 4: (56, 64)}
     image_sum = None
     for k in range(ITERS):
 
         def beside_first(u, k=k):
             if k == 0:
                 rows_loop(*turned[u], 2, turn)
-            elif u == -1:
+            elif u == 0:
                 mix_of(k - 1)
-            elif u == 0:
+            elif u == 1:
                 image_gram_of(k - 1, image_sum.take())
-            elif u == 1:
+            else:
                 small[k - 1, STEP] = spd_solve(small[k - 1, IG], small[k - 1, GG])
 
         fresh = reduce_scatter(sums, plane, r1, p1, r2, tr, beside_first)
@@ -541,15 +571,19 @@
                 grads[k] = grad
                 if k:
                     conj[...] = direction
+            else:
+                cut_unit(v - 1, (0, 1, 3))
             if k == 0:
                 rows_loop(*turned_later[v], 2, turn)
 
         gather_all(vec, plane, tr, beside_second)
         grad_sum.step()
-        lax.fori_loop(0, 16, cut, 0)
-        rows_loop(0, 40, UNROLL, forward(2 * N * k))
+        for v in range(4):
+            cut_unit(v, (2,))
+        gram_acc[...] = jnp.zeros_like(gram_acc)
+        forward_groups(k, 0, 5)
         grad_sum.step()
-        rows_loop(40, ROWS, UNROLL, forward(2 * N * k))
+        forward_groups(k, 5, ROWS // UNROLL)
         last = k + 1 == ITERS
         image_sum = TileSum(
             [in_plane, across_it] if last else [along_x, along_z, across_it],
@@ -587,7 +621,7 @@
 
     def strip(s, carry):
         at = pl.ds(pl.multiple_of(s * width, width), width)
-        out = dot(left, images[:, at], 1, 0)
+        out = dot(left, images[:, pl.ds(pl.multiple_of(LEAD + s * width, width), width)], 1, 0)
         res[:, at] = t_mem[:, at] - (out[:N] + out[N:])
         return carry
 
@@ -620,7 +654,7 @@
                 pltpu.VMEM(chunks, F32),
                 pltpu.VMEM(chunks, F32),
                 pltpu.VMEM((group, 2 * N, B), BF16),
-                pltpu.VMEM((2 * N * ITERS, ROWS * B), BF16),
+                pltpu.VMEM((2 * N * ITERS, LEAD + ROWS * B), BF16),
                 pltpu.VMEM((N, ROWS * B), F32),
                 pltpu.VMEM((ITERS, N, width), F32),
                 pltpu.VMEM((N, width), F32),

time: 174 us -> 168 us (0.966)
  Pallas kernels: 168 us -> 162 us
    pallas_call x1, Pallas kernels: 166 us -> 160 us  [body(): pl.pallas_call(functools.partial(cgls_kernel, n_row, n_col), out_shape=[j...]
where the time goes in v5:
time: 168 us
  Pallas kernels  162 us (96%)
  local copies, waits for them, and re-layouts  4.71 us (3%)
    pallas_call x1, Pallas kernels, body(): pl.pallas_call(functools.partial(cgls_kernel, n_row, n_col), out_shape=[j...  160 us
    unnamed x3, local copies, waits for them, and re-layouts  4.6 us

profile of v5, /device:TPU:1, one launch (start us, length us, event | category | flops | bytes accessed | tf_op | source)
XLA Modules:
  0.0 167.8 jit_solution(9901366047213882786)
XLA Ops:
  0.6 0.8 copy.6
  1.4 0.1 reshape.140
  1.5 0.6 fusion.cols
  2.1 1.5 shard_map.50.table
  3.6 160.3 %shard_map.51 = (f32[32,1024]{1,0:T(8,128)}, f32[32,8192]{1,0:T(8,128)}) custom-call(s32[8,256]{1,0:T(8,128)} %shard_map.50.table, f32[1024,32,128]{2,1,0:T(8,128)} %bitcast.1, f32[32,8192]{1,0:T(8,128)} %targets.1), custom_call_target="tpu_custom_call" | custom-call | tf_op jit(solution)/shard_map/pallas_call | solution.py:644
  164.0 1.6 copy.9
  165.6 2.3 %copy.10 = f32[32,8192]{1,0:T(8,128)} copy(f32[32,8192]{1,0:T(8,128)} %get-tuple-element.5) | data formatting | bytes 2097152

commit v6 on v5

--- a/solution.py
+++ b/solution.py
@@ -84,9 +84,16 @@
     return jnp.concatenate(parts, axis=0)[:, N : 2 * N]
 
 
-def apply_t(square, both):
-    hi, lo = split(square.T)
-    left = jnp.concatenate([jnp.concatenate([hi, hi], axis=1), jnp.concatenate([lo, lo], axis=1)], axis=0)
+def left_of(squares):
+    his, los = [], []
+    for square in squares:
+        hi, lo = split(square.T)
+        his += [hi, hi]
+        los += [lo, lo]
+    return jnp.concatenate([jnp.concatenate(his, axis=1), jnp.concatenate(los, axis=1)], axis=0)
+
+
+def halves_sum(left, both):
     out = dot(left, both, 1, 0)
     return out[:N] + out[N:]
 
@@ -94,10 +101,11 @@
 COL, ORDER, FIRST, LAST, SOME = range(5)
 
 
-def order_kernel(cols, table):
-    count = cols.shape[1]
+def order_kernel(n_col, flat, table):
+    count = flat.shape[1]
+    cols = flat[...] // (CBD * n_col) * CBD + lax.rem(flat[...], CBD)
     shape = (count, count)
-    row = cols[...].astype(F32)
+    row = cols.astype(F32)
     across = jnp.broadcast_to(row, shape)
     down = across.T
     p = lax.broadcasted_iota(jnp.int32, shape, 0).astype(F32)
@@ -109,7 +117,7 @@
     rank = jnp.sum(before, axis=1, keepdims=True)
     alone = jnp.where(jnp.sum(twins, axis=1, keepdims=True) == 0.0, 1.0, 0.0)
     place = rank == q
-    table[COL : COL + 1, :] = cols[...]
+    table[COL : COL + 1, :] = cols
     table[ORDER : ORDER + 1, :] = jnp.sum(jnp.where(place, p, zero), axis=0, keepdims=True).astype(jnp.int32)
     table[FIRST : FIRST + 1, :] = jnp.sum(jnp.where(place, alone, zero), axis=0, keepdims=True).astype(jnp.int32)
     upto = jnp.sum(jnp.where(down <= q, one, zero), axis=0, keepdims=True)
@@ -119,10 +127,11 @@
     table[5:8, :] = jnp.zeros((3, count), jnp.int32)
 
 
-def order_of(cols):
+def order_of(flat, n_col):
     return pl.pallas_call(
-        order_kernel, out_shape=jax.ShapeDtypeStruct((8, cols.shape[1]), jnp.int32)
-    )(cols)
+        functools.partial(order_kernel, n_col),
+        out_shape=jax.ShapeDtypeStruct((8, flat.shape[1]), jnp.int32),
+    )(flat)
 
 
 class Traffic:
@@ -382,7 +391,7 @@
 
 def cgls_kernel(n_row, n_col, table, blocks, targets, sol, res, *scratch):
     across, down, pieces, running, sums, vec, parts, images, t_mem, grads = scratch[:10]
-    conj, gram_acc, small, r1, p1, r2, box, send_sem, recv_sem, load_sem = scratch[10:]
+    conj, gram_acc, small, r1, p1, r2, box, last_box, send_sem, recv_sem, load_sem, out_sem = scratch[10:]
     row, col = lax.axis_index("row"), lax.axis_index("col")
     plane = Plane(row, col)
     along_x, along_z, in_plane, across_it = sum_stages(row, col, n_row, n_col)
@@ -537,12 +546,16 @@
     add_up()
     pl.semaphore_wait(barrier, len(who))
     slot0 = RS_SLOTS + AG_SLOTS
+    width = 1024
+    strips = ROWS * B // width
     turned = {0: (0, 10), 1: (10, 22), 2: (22, 32)}
     turned_later = {0: (32, 36), 1: (36, 46), 2: (46, 52), 3: (52, 56), 4: (56, 64)}
     image_sum = None
     for k in range(ITERS):
 
-        def beside_first(u, k=k):
+        ready = []
+
+        def beside_first(u, k=k, ready=ready):
             if k == 0:
                 rows_loop(*turned[u], 2, turn)
             elif u == 0:
@@ -550,14 +563,21 @@
             elif u == 1:
                 image_gram_of(k - 1, image_sum.take())
             else:
-                small[k - 1, STEP] = spd_solve(small[k - 1, IG], small[k - 1, GG])
+                step = spd_solve(small[k - 1, IG], small[k - 1, GG])
+                small[k - 1, STEP] = step
+                left = left_of([step])
+                ready.append(left)
+                if k == 1:
+                    ready.append(grads[0])
+                else:
+                    known = halves_sum(left_of([small[1, MIX]]), stacked(conj[...]))
+                    ready.append(grads[1] - halves_sum(left, stacked(known)))
 
         fresh = reduce_scatter(sums, plane, r1, p1, r2, tr, beside_first)
         if k == 0:
             grad = fresh
         else:
-            direction = fresh if k == 1 else fresh + apply_t(small[1, MIX], stacked(conj[...]))
-            grad = grads[k - 1] - apply_t(small[k - 1, STEP], stacked(direction))
+            grad = ready[1] - halves_sum(ready[0], stacked(fresh))
         for h in range(2):
             for j in range(4):
                 at = (4 * h + j) * B
@@ -569,8 +589,8 @@
                 both = stacked(grad)
                 grad_sum.put(pack(fold(dot(both, both, 1, 1))))
                 grads[k] = grad
-                if k:
-                    conj[...] = direction
+                if k == 1:
+                    conj[...] = fresh
             else:
                 cut_unit(v - 1, (0, 1, 3))
             if k == 0:
@@ -589,7 +609,7 @@
             [in_plane, across_it] if last else [along_x, along_z, across_it],
             tr_small,
             slot0 + (2 * k + 1) * SUM_SLOTS,
-            box.at[2 * k + 1],
+            last_box if last else box.at[2 * k + 1],
             8 * (k + 1),
         )
         image_sum.put(image_grams(k))
@@ -603,29 +623,52 @@
         else:
             small[k, GG] = unpack(grad_sum.take())
             mix_of(k)
+            mix = small[2, MIX]
+            now = small[1, STEP]
+            ahead = [exact(small[1, MIX], mix), mix]
+            upto = [small[0, STEP] + exact(small[1, MIX], now), now]
+            left = jnp.concatenate([left_of(ahead), left_of(upto)], axis=0)
+            out = dot(left, jnp.concatenate([stacked(grads[j]) for j in range(2)], axis=0), 1, 0)
+            grads[2] = grads[2] + (out[:N] + out[N : 2 * N])
+            conj[...] = out[2 * N : 3 * N] + out[3 * N :]
+
+            def prepare(s, carry, left=left):
+                at = pl.ds(pl.multiple_of(s * width, width), width)
+                there = pl.ds(pl.multiple_of(LEAD + s * width, width), width)
+                out = dot(left, images[0 : 4 * N, there], 1, 0)
+                own = images[4 * N : 5 * N, there].astype(F32) + images[5 * N : 6 * N, there].astype(F32)
+                images[4 * N : 6 * N, there] = stacked(own + (out[:N] + out[N : 2 * N]))
+                t_mem[:, at] = t_mem[:, at] - (out[2 * N : 3 * N] + out[3 * N :])
+                return carry
+
+            lax.fori_loop(0, ROWS * B // width, prepare, 0)
             image_sum.step()
             image_gram_of(k, image_sum.take())
 
-    e2 = spd_solve(small[2, IG], small[2, GG])
-    e1 = small[1, STEP] + exact(small[2, MIX], e2)
-    e0 = small[0, STEP] + exact(small[1, MIX], e1)
-    his, los = [], []
-    for e in (e0, e1, e2):
-        hi, lo = split(e.T)
-        his += [hi, hi]
-        los += [lo, lo]
-    left = jnp.concatenate([jnp.concatenate(his, axis=1), jnp.concatenate(los, axis=1)], axis=0)
-    out = dot(left, jnp.concatenate([stacked(grads[j]) for j in range(3)], axis=0), 1, 0)
-    sol[...] = out[:N] + out[N:]
-    width = 1024
-
-    def strip(s, carry):
+    left = left_of([spd_solve(small[2, IG], small[2, GG])])
+    conj[...] = conj[...] + halves_sum(left, stacked(grads[2]))
+    out_sol = pltpu.make_async_copy(conj, sol, out_sem.at[strips])
+    out_sol.start()
+
+    def write(s):
         at = pl.ds(pl.multiple_of(s * width, width), width)
-        out = dot(left, images[:, pl.ds(pl.multiple_of(LEAD + s * width, width), width)], 1, 0)
-        res[:, at] = t_mem[:, at] - (out[:N] + out[N:])
+        return pltpu.make_async_copy(t_mem.at[:, at], res.at[:, at], out_sem.at[s])
+
+    def finish(s, carry):
+        at = pl.ds(pl.multiple_of(s * width, width), width)
+        there = pl.ds(pl.multiple_of(LEAD + s * width, width), width)
+        t_mem[:, at] = t_mem[:, at] - halves_sum(left, images[4 * N : 6 * N, there])
+        write(s).start()
         return carry
 
-    lax.fori_loop(0, ROWS * B // width, strip, 0)
+    lax.fori_loop(0, strips, finish, 0)
+    out_sol.wait()
+
+    def wait(s, carry):
+        write(s).wait()
+        return carry
+
+    lax.fori_loop(0, strips, wait, 0)
     tr_small.finish()
 
 
@@ -633,9 +676,7 @@
     n_row = lax.axis_size("row")
     n_col = lax.axis_size("col")
     group = CBD * n_row
-    flat = block_cols.reshape(1, -1)
-    table = order_of(flat // (CBD * n_col) * CBD + lax.rem(flat, CBD))
-    vmem = pl.BlockSpec(memory_space=pltpu.VMEM)
+    table = order_of(block_cols.reshape(1, -1), n_col)
     anywhere = pl.BlockSpec(memory_space=pl.ANY)
     width = CBD * B
     chunks = (4, 4, 2, CBD // 2, N, B)
@@ -645,7 +686,7 @@
             functools.partial(cgls_kernel, n_row, n_col),
             out_shape=[jax.ShapeDtypeStruct((N, width), F32), jax.ShapeDtypeStruct(targets.shape, F32)],
             in_specs=[pl.BlockSpec(memory_space=pltpu.SMEM), anywhere, anywhere],
-            out_specs=[vmem] * 2,
+            out_specs=[anywhere] * 2,
             scratch_shapes=[
                 pltpu.VMEM((ROWS, 2 * B, 4 * B), BF16),
                 pltpu.VMEM((ROWS, 4 * B, 2 * B), BF16),
@@ -663,10 +704,12 @@
                 pltpu.VMEM((2, 4, 6, 2, N, B), F32),
                 pltpu.VMEM((2, 4, 4, N, B), F32),
                 pltpu.VMEM((2, 6, 2, N, B), F32),
-                pltpu.VMEM((6, 3, n_row, 24, B), F32),
+                pltpu.VMEM((5, 3, n_col, 16, B), F32),
+                pltpu.VMEM((2, n_row, 24, B), F32),
                 pltpu.SemaphoreType.DMA((slots,)),
                 pltpu.SemaphoreType.DMA((slots,)),
                 pltpu.SemaphoreType.DMA((SLOTS + 1,)),
+                pltpu.SemaphoreType.DMA((ROWS * B // 1024 + 1,)),
             ],
             compiler_params=pltpu.CompilerParams(
                 collective_id=0, has_side_effects=True, vmem_limit_bytes=60 * MIB

time: 168 us -> 166 us (0.988)
  Pallas kernels: 162 us -> 160 us
    pallas_call x1, Pallas kernels: 160 us -> 158 us  [body(): pl.pallas_call(functools.partial(cgls_kernel, n_row, n_col), out_shape=[j...]
where the time goes in v6:
time: 166 us
  Pallas kernels  160 us (96%)
  local copies, waits for them, and re-layouts  5.27 us (3%)
    pallas_call x1, Pallas kernels, body(): pl.pallas_call(functools.partial(cgls_kernel, n_row, n_col), out_shape=[j...  158 us
    unnamed x3, local copies, waits for them, and re-layouts  4.6 us

profile of v6, /device:TPU:1, one launch (start us, length us, event | category | flops | bytes accessed | tf_op | source)
XLA Modules:
  0.0 165.9 jit_solution(11105228271021096926)
XLA Ops:
  0.6 0.8 copy.6
  1.4 0.7 reshape.10.flat
  2.1 1.6 shard_map.50.table
  3.6 158.5 %shard_map.51 = (f32[32,1024]{1,0:T(8,128)}, f32[32,8192]{1,0:T(8,128)}) custom-call(s32[8,256]{1,0:T(8,128)} %shard_map.50.table, f32[1024,32,128]{2,1,0:T(8,128)} %bitcast.1, f32[32,8192]{1,0:T(8,128)} %targets.1), custom_call_target="tpu_custom_call" | custom-call | tf_op jit(solution)/shard_map/pallas_call | solution.py:685
  162.1 1.6 copy.9
  163.7 2.3 %copy.10 = f32[32,8192]{1,0:T(8,128)} copy(f32[32,8192]{1,0:T(8,128)} %get-tuple-element.5) | data formatting | bytes 2097152

commit v7 on v6

--- a/solution.py
+++ b/solution.py
@@ -337,12 +337,9 @@
 
 
 def sum_stages(row, col, n_row, n_col):
-    z, x = row // 4, lax.rem(row, 4)
-    along_x = ([(z * 4 + lax.rem(x + d, 4), col) for d in range(1, 4)], x, 4)
-    along_z = ([(lax.rem(z + d, 4) * 4 + x, col) for d in range(1, 4)], z, 4)
     plane = ([(lax.rem(row + d, n_row), col) for d in range(1, n_row)], row, n_row)
     across = ([(row, lax.rem(col + d, n_col)) for d in range(1, n_col)], col, n_col)
-    return along_x, along_z, plane, across
+    return plane, across
 
 
 class TileSum:
@@ -391,10 +388,10 @@
 
 def cgls_kernel(n_row, n_col, table, blocks, targets, sol, res, *scratch):
     across, down, pieces, running, sums, vec, parts, images, t_mem, grads = scratch[:10]
-    conj, gram_acc, small, r1, p1, r2, box, last_box, send_sem, recv_sem, load_sem, out_sem = scratch[10:]
+    conj, gram_acc, small, r1, p1, r2, box, send_sem, recv_sem, load_sem, out_sem = scratch[10:]
     row, col = lax.axis_index("row"), lax.axis_index("col")
     plane = Plane(row, col)
-    along_x, along_z, in_plane, across_it = sum_stages(row, col, n_row, n_col)
+    in_plane, across_it = sum_stages(row, col, n_row, n_col)
     tr, tr_small = Traffic(send_sem, recv_sem), Traffic(send_sem, recv_sem)
 
     size = LOAD * 16
@@ -582,7 +579,7 @@
             for j in range(4):
                 at = (4 * h + j) * B
                 vec[plane.z, plane.x, h, j] = grad[:, at : at + B]
-        grad_sum = TileSum([across_it, along_x, along_z], tr_small, slot0 + 2 * k * SUM_SLOTS, box.at[2 * k], 8)
+        grad_sum = TileSum([across_it, in_plane], tr_small, slot0 + 2 * k * SUM_SLOTS, box.at[2 * k], 8)
 
         def beside_second(v, k=k):
             if v == 0:
@@ -601,23 +598,19 @@
         for v in range(4):
             cut_unit(v, (2,))
         gram_acc[...] = jnp.zeros_like(gram_acc)
-        forward_groups(k, 0, 5)
-        grad_sum.step()
-        forward_groups(k, 5, ROWS // UNROLL)
+        forward_groups(k, 0, ROWS // UNROLL)
         last = k + 1 == ITERS
         image_sum = TileSum(
-            [in_plane, across_it] if last else [along_x, along_z, across_it],
+            [in_plane, across_it],
             tr_small,
             slot0 + (2 * k + 1) * SUM_SLOTS,
-            last_box if last else box.at[2 * k + 1],
+            box.at[2 * k + 1],
             8 * (k + 1),
         )
         image_sum.put(image_grams(k))
         if not last:
-            rows_loop(0, 40, UNROLL, backward(2 * N * k))
             small[k, GG] = unpack(grad_sum.take())
-            image_sum.step()
-            rows_loop(40, ROWS, UNROLL, backward(2 * N * k))
+            rows_loop(0, ROWS, UNROLL, backward(2 * N * k))
             add_up()
             image_sum.step()
         else:
@@ -704,8 +697,7 @@
                 pltpu.VMEM((2, 4, 6, 2, N, B), F32),
                 pltpu.VMEM((2, 4, 4, N, B), F32),
                 pltpu.VMEM((2, 6, 2, N, B), F32),
-                pltpu.VMEM((5, 3, n_col, 16, B), F32),
-                pltpu.VMEM((2, n_row, 24, B), F32),
+                pltpu.VMEM((6, 2, n_row, 24, B), F32),
                 pltpu.SemaphoreType.DMA((slots,)),
                 pltpu.SemaphoreType.DMA((slots,)),
                 pltpu.SemaphoreType.DMA((SLOTS + 1,)),

time: 166 us -> 163 us (0.982)
  Pallas kernels: 160 us -> 157 us
    pallas_call x1, Pallas kernels: 158 us -> 155 us  [body(): pl.pallas_call(functools.partial(cgls_kernel, n_row, n_col), out_shape=[j...]
where the time goes in v7:
time: 163 us
  Pallas kernels  157 us (96%)
  local copies, waits for them, and re-layouts  5.27 us (3%)
    pallas_call x1, Pallas kernels, body(): pl.pallas_call(functools.partial(cgls_kernel, n_row, n_col), out_shape=[j...  155 us
    unnamed x3, local copies, waits for them, and re-layouts  4.6 us

profile of v7, /device:TPU:1, one launch (start us, length us, event | category | flops | bytes accessed | tf_op | source)
XLA Modules:
  0.0 162.8 jit_solution(6949862768165661670)
XLA Ops:
  0.6 0.8 copy.6
  1.4 0.7 reshape.10.flat
  2.1 1.6 shard_map.50.table
  3.6 155.3 %shard_map.51 = (f32[32,1024]{1,0:T(8,128)}, f32[32,8192]{1,0:T(8,128)}) custom-call(s32[8,256]{1,0:T(8,128)} %shard_map.50.table, f32[1024,32,128]{2,1,0:T(8,128)} %bitcast.1, f32[32,8192]{1,0:T(8,128)} %targets.1), custom_call_target="tpu_custom_call" | custom-call | tf_op jit(solution)/shard_map/pallas_call | solution.py:678
  158.9 1.6 copy.9
  160.5 2.3 %copy.10 = f32[32,8192]{1,0:T(8,128)} copy(f32[32,8192]{1,0:T(8,128)} %get-tuple-element.5) | data formatting | bytes 2097152
